TPU v7x, 256 devices: a whole 4x4x8 slice. The times are simulated.
256 devices in a mesh: dp: 32 (over y, x, core), tensor: 8 (over z).
Axes of the slice: x: 4, y: 4, z: 8, core: 2. Of those that a mesh axis runs over, the one named last changes fastest.
Arguments:
- layer_out: bfloat16 [256, 5120], P('dp', 'tensor'), may hold values from -140 to 140
- resid_mid: bfloat16 [256, 5120], P('dp', 'tensor'), may hold values from -140 to 140
- final_gain: float32 [5120], replicated, may hold values from 0.5 to 1.5
- mlp_gain: float32 [5120], replicated, may hold values from 0.5 to 1.5
- head_weight: bfloat16 [98304, 5120], P(('tensor', 'dp')), may hold values from -0.28125 to 0.28125
- w_gate: bfloat16 [16384, 5120], P(('tensor', 'dp')), may hold values from -0.078125 to 0.078125
- w_up: bfloat16 [16384, 5120], P(('tensor', 'dp')), may hold values from -0.078125 to 0.078125
- w_down: bfloat16 [16384, 5120], P(('tensor', 'dp')), may hold values from -0.046875 to 0.046875
- teacher_logits: bfloat16 [256, 98304], P('dp', 'tensor'), may hold values from -15 to 15
- assign: int32 [32, 8], P('dp'), may hold values from 0 to 7, each once within a row
- lengths: int32 [32, 2], P('dp'), may hold values from 1 to 4
- token_ids: int32 [256], P('dp'), may hold values from 0 to 98303
Outputs:
- grad_resid: bfloat16 [256, 5120], P('dp', 'tensor')
- grad_head: bfloat16 [98304, 5120], P(('tensor', 'dp'))
- grad_gate: bfloat16 [16384, 5120], P(('tensor', 'dp'))
- grad_up: bfloat16 [16384, 5120], P(('tensor', 'dp'))
- grad_down: bfloat16 [16384, 5120], P(('tensor', 'dp'))
Inputs may be any that keep to these rules, and one draw needn't show every extreme that they name: `assign`: each row is a permutation of the 8 slots.
All inputs are finite; a program needn't handle non-finite values.
Results may differ from a plain program's by a relative error of at most 0.02.
Values may be sent and summed in bfloat16 or wider, within the bound.
A program may use at most 128 MiB of HBM per device.

v0:
```python
import jax
import jax.numpy as jnp
from jax import lax
from jax.sharding import PartitionSpec as P

D = 5120
SLOT = 4


EPS = 1e-06
CE_WEIGHT = 0.5
LOSS_SCALE = 4096.0


def rms_scale(values):
    return lax.rsqrt(jnp.mean(values * values, axis=-1, keepdims=True) + EPS)


def norm_back(values, gain_vector, out_grads):
    row_scale = rms_scale(values)
    weighted = gain_vector * out_grads
    inner_sum = jnp.sum(values * weighted, axis=-1, keepdims=True) / values.shape[-1]
    return row_scale * weighted - values * row_scale**3 * inner_sum


def contract_rows(left, right):
    return lax.dot_general(
        left, right, (((0,), (0,)), ((), ())), preferred_element_type=jnp.float32
    )


def contract_cols(left, right):
    return lax.dot_general(
        left, right, (((1,), (1,)), ((), ())), preferred_element_type=jnp.float32
    )


def per_device(
    layer_out,
    resid_mid,
    final_gain,
    mlp_gain,
    head_weight,
    w_gate,
    w_up,
    w_down,
    teacher_logits,
    assign,
    lengths,
    token_ids,
):
    rows_local = layer_out.shape[0]
    cols_local = layer_out.shape[1]
    group_index = lax.axis_index("dp")
    shard_index = lax.axis_index("tensor")
    group_count = lax.axis_size("dp")
    row_start = group_index * rows_local
    col_start = shard_index * cols_local
    out_cols, mid_cols = (
        lax.all_gather(layer_out, "tensor", axis=1, tiled=True),
        lax.all_gather(resid_mid, "tensor", axis=1, tiled=True),
    )
    out_all, mid_all, length_all, ids_all = (
        lax.all_gather(out_cols, "dp", axis=0, tiled=True),
        lax.all_gather(mid_cols, "dp", axis=0, tiled=True),
        lax.all_gather(lengths, "dp", axis=0, tiled=True),
        lax.all_gather(token_ids, "dp", axis=0, tiled=True),
    )
    picked = jnp.take(teacher_logits, assign[0], axis=0)
    teacher = lax.all_to_all(picked, "dp", split_axis=1, concat_axis=0, tiled=True).astype(
        jnp.float32
    )
    out_wide = out_all.astype(jnp.float32)
    final_rows = (out_wide * rms_scale(out_wide) * final_gain).astype(jnp.bfloat16)
    logits = contract_cols(final_rows, head_weight)
    local_max = jnp.max(logits, axis=1)
    global_max = lax.pmax(local_max, ("dp", "tensor"))
    expd = jnp.exp(logits - global_max[:, None])
    totals, moments = lax.psum(
        (jnp.sum(expd, axis=1), jnp.sum(expd * (logits - teacher), axis=1)), ("dp", "tensor")
    )
    probs_all = expd / totals[:, None]
    slot_index = jnp.arange(SLOT, dtype=jnp.int32)
    live_mask = (slot_index[None, None, :] < length_all[:, :, None]).reshape(-1).astype(jnp.float32)
    live_count = jnp.sum(length_all).astype(jnp.float32)
    token_weight = live_mask * (LOSS_SCALE / live_count)
    vocab_local = head_weight.shape[0]
    vocab_start = (shard_index * group_count + group_index) * vocab_local
    target = (
        ids_all[:, None] - vocab_start == jnp.arange(vocab_local, dtype=jnp.int32)[None, :]
    ).astype(jnp.float32)
    dlogits = token_weight[:, None] * (
        probs_all * (logits - teacher - (moments / totals)[:, None] + CE_WEIGHT)
        - CE_WEIGHT * target
    )
    dlog_b = dlogits.astype(jnp.bfloat16)
    grad_head = contract_rows(dlog_b, final_rows).astype(jnp.bfloat16)
    dfinal = lax.psum(
        jnp.dot(dlog_b, head_weight, preferred_element_type=jnp.float32), ("dp", "tensor")
    )
    grad_out = norm_back(out_wide, final_gain, dfinal)
    grad_out_b = grad_out.astype(jnp.bfloat16)
    grad_out_own = lax.dynamic_slice(grad_out, (row_start, col_start), (rows_local, cols_local))
    mid_wide = mid_all.astype(jnp.float32)
    normed = (mid_wide * rms_scale(mid_wide) * mlp_gain).astype(jnp.bfloat16)
    gate_pre = contract_cols(normed, w_gate)
    up_pre = contract_cols(normed, w_up)
    gate_sigmoid = jax.nn.sigmoid(gate_pre)
    activated = (gate_pre * gate_sigmoid * up_pre).astype(jnp.bfloat16)
    act_grad = contract_cols(grad_out_b, w_down)
    grad_down = contract_rows(activated, grad_out_b).astype(jnp.bfloat16)
    up_grad = (act_grad * gate_pre * gate_sigmoid).astype(jnp.bfloat16)
    gate_grad = (act_grad * up_pre * gate_sigmoid * (1.0 + gate_pre * (1.0 - gate_sigmoid))).astype(
        jnp.bfloat16
    )
    grad_gate = contract_rows(gate_grad, normed).astype(jnp.bfloat16)
    grad_up = contract_rows(up_grad, normed).astype(jnp.bfloat16)
    mlp_partial = lax.psum_scatter(
        (
            jnp.dot(gate_grad, w_gate, preferred_element_type=jnp.float32)
            + jnp.dot(up_grad, w_up, preferred_element_type=jnp.float32)
        ).astype(jnp.bfloat16),
        "dp",
        scatter_dimension=0,
        tiled=True,
    )
    normed_grad_own = lax.psum_scatter(
        mlp_partial, "tensor", scatter_dimension=1, tiled=True
    ).astype(jnp.float32)
    mid_rows = lax.dynamic_slice_in_dim(mid_wide, row_start, rows_local, 0)
    mid_own = lax.dynamic_slice_in_dim(mid_rows, col_start, cols_local, 1)
    mlp_gain_own = lax.dynamic_slice_in_dim(mlp_gain, col_start, cols_local, 0)
    mid_scale = rms_scale(mid_rows)
    mid_weighted = mlp_gain_own * normed_grad_own
    mid_inner = lax.psum(jnp.sum(mid_own * mid_weighted, axis=1, keepdims=True), "tensor") / D
    grad_resid = (
        grad_out_own + mid_scale * mid_weighted - mid_own * mid_scale**3 * mid_inner
    ).astype(jnp.bfloat16)
    return (grad_resid, grad_head, grad_gate, grad_up, grad_down)


def solution(mesh):
    return jax.shard_map(
        per_device,
        mesh=mesh,
        in_specs=(
            P("dp", "tensor"),
            P("dp", "tensor"),
            P(),
            P(),
            P(("tensor", "dp"), None),
            P(("tensor", "dp"), None),
            P(("tensor", "dp"), None),
            P(("tensor", "dp"), None),
            P("dp", "tensor"),
            P("dp", None),
            P("dp", None),
            P("dp"),
        ),
        out_specs=(
            P("dp", "tensor"),
            P(("tensor", "dp"), None),
            P(("tensor", "dp"), None),
            P(("tensor", "dp"), None),
            P(("tensor", "dp"), None),
        ),
        check_vma=False,
    )
```

profile of v0, /device:TPU:1, one launch (start us, length us, event | category | flops | bytes accessed | tf_op | source)
XLA Modules:
  0.0 702.3 jit_solution(14159829048628449964)
XLA Ops:
  7.2 25.3 %all_gather.18 = bf16[8,5120]{1,0:T(8,128)(2,1)} all-gather(bf16[8,640]{1,0:T(8,128)(2,1)} %param.12), channel_id=1, replica_groups=mesh['dp'=32,'tensor'=8] {'tensor'}, dimensions={1}, use_global_device_ids=true | all-gather | bytes 92160 | tf_op jit(solution)/shard_map/all_gather | solution.py:60
  32.6 20.3 %all_gather.22 = bf16[8,5120]{1,0:T(8,128)(2,1)} all-gather(bf16[8,640]{1,0:T(8,128)(2,1)} %param.13), channel_id=1, replica_groups=mesh['dp'=32,'tensor'=8] {'tensor'}, dimensions={1}, use_global_device_ids=true | all-gather | bytes 92160 | tf_op jit(solution)/shard_map/all_gather | solution.py:61
  52.9 0.7 fusion.15
  53.6 1.8 gather_fusion
  55.4 0.7 compare_and_fusion
  56.0 0.8 broadcast_select_fusion
  56.8 20.2 %all-to-all-start = ((bf16[8,32,384]{2,0,1:T(8,128)(2,1)}), bf16[8,32,384]{2,0,1:T(8,128)(2,1)S(1)}, u32[]{:S(2)}, u32[]{:S(2)}) async-start(bf16[8,32,384]{2,0,1:T(8,128)(2,1)} %broadcast_select_fusion), calls=%async_computation | async-start | bytes 393216 | tf_op jit(solution)/shard_map/all_to_all | solution.py:70
  77.1 21.8 %all-gather = s32[32,1,2]{2,1,0:T(1,128)S(1)} all-gather(s32[1,1,2]{2,1,0:T(1,128)} %bitcast.43), channel_id=1, replica_groups=mesh['dp'=32,'tensor'=8] {'dp'}, dimensions={0}, use_global_device_ids=true | all-gather | bytes 264 | tf_op jit(solution)/shard_map/all_gather | solution.py:66
  98.9 0.7 reduce_sum.77
  100.4 0.1 mul.176
  100.5 1.3 dynamic-slice
  102.4 0.9 dynamic-update-slice
  103.3 11.3 %all-reduce = s32[256]{0:T(256)S(1)} all-reduce(s32[256]{0:T(256)S(1)} %dynamic-update-slice), channel_id=1, replica_groups=mesh['dp'=32,'tensor'=8] {'dp'}, use_global_device_ids=true, to_apply=%add | all-reduce | flops 256 | bytes 2048
  114.7 2.3 fusion.1
  117.0 0.6 multiply_multiply_fusion
  117.6 4.6 fusion.20
  122.1 76.9 %pmax.7 = f32[256]{0:T(256)S(1)} all-reduce(f32[256]{0:T(256)S(1)} %get-tuple-element.15), channel_id=1, replica_groups=mesh['dp'=32,'tensor'=8] {'dp','tensor'}, use_global_device_ids=true, to_apply=%region_3.4 | all-reduce | flops 256 | bytes 2048 | tf_op jit(solution)/shard_map/pmax | solution.py:77
  199.0 0.2 fusion.13
  199.2 72.7 %all-reduce.1 = (f32[256]{0:T(256)S(1)}, f32[256]{0:T(256)S(1)}) all-reduce(f32[256]{0:T(256)S(1)} %get-tuple-element.6, f32[256]{0:T(256)S(1)} %get-tuple-element.5), channel_id=1, replica_groups=mesh['dp'=32,'tensor'=8] {'dp','tensor'}, use_global_device_ids=true, to_apply=%region_7.8 | all-reduce | flops 512 | bytes 4096 | tf_op jit(solution)/shard_map/psum | solution.py:79
  271.9 6.1 fusion.17
  278.1 0.2 reduce-scatter.5.cloned.1.call-start
  278.4 2.5 multiply_reduce_fusion
  280.9 3.0 fusion.19
  284.0 2.3 fusion.18
  286.3 258.1 %all-reduce.4.cloned.1.call-done = f32[256,5120]{1,0:T(8,128)} async-done(((f32[256,5120]{1,0:T(8,128)}), f32[256,5120]{1,0:T(8,128)}) %all-reduce.4.cloned.1.call-update) | async-done | bytes 5242896 | tf_op jit(solution)/shard_map/psum | solution.py:98
  544.4 3.4 fusion.6
  547.8 0.6 copy-done.3
  548.5 1.6 fusion.5
  550.1 0.9 multiply_convert_fusion.3
  551.1 1.1 copy-done.14
  552.2 0.9 fusion.21
  553.1 2.3 fusion
  555.4 0.8 dynamic_slice.14
  556.2 2.4 convert_element_type.69
  558.6 2.3 copy-done.7
  561.0 0.2 multiply_reduce_fusion.2
  561.1 0.6 add_rsqrt_fusion.2
  561.7 4.5 convolution_convert_fusion
  566.3 1.8 convolution_convert_fusion.2
  568.1 1.4 convolution_convert_fusion.1
  569.5 71.7 %reduce-scatter.5.cloned.1.call-done = bf16[8,5120]{1,0:T(8,128)(2,1)} async-done(((bf16[256,5120]{1,0:T(8,128)(2,1)}), bf16[8,5120]{1,0:T(8,128)(2,1)}) %reduce-scatter.5.cloned.1.call-update) | async-done | bytes 81936 | tf_op jit(solution)/shard_map/reduce_scatter | solution.py:118
  641.2 2.4 copy.24
  643.6 1.8 convolution_convert_fusion.3
  645.4 34.7 %reduce-scatter.7.cloned.1.call-done = bf16[640,8]{1,0:T(8,128)(2,1)} async-done(((bf16[5120,8]{1,0:T(8,128)(2,1)}), bf16[640,8]{1,0:T(8,128)(2,1)}) %reduce-scatter.7.cloned.1.call-update) | async-done | bytes 10256
  680.1 1.0 copy.25
  681.1 1.0 multiply_reduce_fusion.3
  682.2 12.1 %psum.31 = f32[8,1]{0,1:T(1,128)S(1)} all-reduce(f32[8,1]{0,1:T(1,128)S(1)} %bitcast.42), channel_id=1, replica_groups=mesh['dp'=32,'tensor'=8] {'tensor'}, use_global_device_ids=true, to_apply=%region_15.16 | all-reduce | flops 8 | bytes 64 | tf_op jit(solution)/shard_map/psum | solution.py:135
  694.2 1.5 subtract_convert_fusion
  (86 shorter events, 0.6 us)
Async XLA Ops:
  7.2 276.8 %copy-start = (bf16[64,5120]{1,0:T(8,128)(2,1)S(1)}, bf16[64,5120]{1,0:T(8,128)(2,1)}, u32[]{:S(2)}) copy-start(bf16[64,5120]{1,0:T(8,128)(2,1)} %param.17) | copy-start | bytes 1966084
  7.2 110.4 %copy-start.18 = (f32[5120]{0:T(1024)S(1)}, f32[5120]{0:T(1024)}, u32[]{:S(2)}) copy-start(f32[5120]{0:T(1024)} %param.14) | copy-start | bytes 61444
  7.2 107.5 %all-gather.4.cloned.1.call-start = ((), (), s32[]{:S(2)}) async-start(), calls=%async_computation.3 | async-start | bytes 2703360 | tf_op jit(solution)/shard_map/all_gather | solution.py:64
  32.6 245.8 %all-gather.6.cloned.1.call-start = ((), (), s32[]{:S(2)}) async-start(), calls=%async_computation.5 | async-start | bytes 2703360 | tf_op jit(solution)/shard_map/all_gather | solution.py:65
  56.8 142.2 %all-to-all-start = ((bf16[8,32,384]{2,0,1:T(8,128)(2,1)}), bf16[8,32,384]{2,0,1:T(8,128)(2,1)S(1)}, u32[]{:S(2)}, u32[]{:S(2)}) async-start(bf16[8,32,384]{2,0,1:T(8,128)(2,1)} %broadcast_select_fusion), calls=%async_computation | async-start | bytes 393216 | tf_op jit(solution)/shard_map/all_to_all | solution.py:70
  77.0 467.4 %all-reduce.4.cloned.1.call-start = ((), (), s32[]{:S(2)}) async-start(), calls=%async_computation.4 | async-start | bytes 10485760 | tf_op jit(solution)/shard_map/psum | solution.py:98
  114.6 157.3 %copy-start.22 = (s32[256]{0:T(256)}, s32[256]{0:T(256)S(1)}, u32[]{:S(2)}) copy-start(s32[256]{0:T(256)S(1)} %broadcast_subtract_fusion) | copy-start | bytes 3076
  117.6 430.3 %copy-start.23 = (f32[256]{0:T(256)}, f32[256]{0:T(256)S(1)}, u32[]{:S(2)}) copy-start(f32[256]{0:T(256)S(1)} %get-tuple-element.12) | copy-start | bytes 3076
  122.1 156.0 %copy-start.8 = (f32[256,384]{1,0:T(8,128)}, f32[256,384]{1,0:T(8,128)S(1)}, u32[]{:S(2)}) copy-start(f32[256,384]{1,0:T(8,128)S(1)} %get-tuple-element.16) | copy-start | bytes 1179652
  271.9 6.1 copy-start.21
  278.1 363.1 %reduce-scatter.5.cloned.1.call-start = ((), (), s32[]{:S(2)}) async-start(), calls=%async_computation.6 | async-start | bytes 2703360 | tf_op jit(solution)/shard_map/reduce_scatter | solution.py:118
  278.4 5.6 copy-start.4
  280.9 3.0 copy-start.25
  280.9 263.5 %copy-start.2 = (bf16[256,5120]{1,0:T(8,128)(2,1)S(1)}, bf16[256,5120]{1,0:T(8,128)(2,1)}, u32[]{:S(2)}) copy-start(bf16[256,5120]{1,0:T(8,128)(2,1)} %all-gather.4.cloned.1.call-done) | copy-start | bytes 7864324
  544.4 4.1 copy-start.3
  544.4 4.1 copy-start.19
  544.4 4.1 copy-start.24
  548.5 1.6 copy-start.11
  548.5 1.6 copy-start.12
  550.1 2.9 copy-start.1
  550.1 2.9 copy-start.10
  551.0 1.1 copy-start.14
  551.0 2.0 copy-start.16
  555.4 124.8 %reduce-scatter.7.cloned.1.call-start = ((), (), s32[]{:S(2)}) async-start(), calls=%async_computation.7 | async-start | bytes 1474560
  556.2 5.5 copy-start.9
  556.2 5.5 copy-start.20
  558.6 2.3 copy-start.7
  561.0 5.3 copy-start.5
  561.0 5.3 copy-start.17
  561.0 5.3 copy-start.26
  561.0 5.3 copy-start.28
  561.1 6.9 slice-start
  561.7 6.3 slice-start.1
  561.7 6.3 copy-start.13
  568.0 75.6 %copy-start.6 = (bf16[256,5120]{1,0:T(8,128)(2,1)S(1)}, bf16[256,5120]{1,0:T(8,128)(2,1)}, u32[]{:S(2)}) copy-start(bf16[256,5120]{1,0:T(8,128)(2,1)} %all-gather.6.cloned.1.call-done) | copy-start | bytes 7864324
  568.0 75.6 %copy-start.15 = (bf16[256,64]{0,1:T(8,128)(2,1)S(1)}, bf16[256,64]{0,1:T(8,128)(2,1)}, u32[]{:S(2)}) copy-start(bf16[256,64]{0,1:T(8,128)(2,1)} %copy-done.14) | copy-start | bytes 98308
  568.1 75.6 %copy-start.27 = (f32[256]{0:T(256)S(1)}, f32[256]{0:T(256)}, u32[]{:S(2)}) copy-start(f32[256]{0:T(256)} %copy-done.25) | copy-start | bytes 3076
  568.1 75.6 %copy-start.29 = (f32[5120]{0:T(1024)S(1)}, f32[5120]{0:T(1024)}, u32[]{:S(2)}) copy-start(f32[5120]{0:T(1024)} %param.15) | copy-start | bytes 61444
  569.5 124.7 %copy-start.30 = (f32[8]{0:T(128)S(1)}, f32[8]{0:T(128)}, u32[]{:S(2)}) copy-start(f32[8]{0:T(128)} %get-tuple-element.13) | copy-start | bytes 100
  569.5 124.7 %copy-start.31 = (f32[8]{0:T(128)S(1)}, f32[8]{0:T(128)}, u32[]{:S(2)}) copy-start(f32[8]{0:T(128)} %get-tuple-element.14) | copy-start | bytes 100
Sparse Core Ops, SparseCore 0:
  32.7 56.5 all-gather.3
  91.8 48.3 all-gather.5
  278.2 266.1 all-reduce.3
  555.5 85.6 reduce-scatter.4
  643.7 36.3 reduce-scatter.6
where the time goes:
time: 710 us; the launch traced here: 702 us
  waiting for transfers between devices  365 us (51%)
  blocking collectives  240 us (34%)
  matrix products  29.6 us (4%)
  starting transfers between devices  20.6 us (3%)
  other arithmetic  19.2 us (3%)
  between operations  15.5 us (2%)
  local copies, waits for them, and re-layouts  12.4 us (2%)
    psum x1, waiting for transfers between devices, per_device(): lax.psum(jnp.dot(dlog_b, head_weight, preferred_element_type=jnp.float32)...  258 us
    pmax x1, blocking collectives, per_device(): global_max = lax.pmax(local_max, ('dp', 'tensor'))  76.9 us
    psum x1, blocking collectives, per_device(): lax.psum((jnp.sum(expd, axis=1), jnp.sum(expd * (logits - teacher), axis=...  72.7 us
    reduce_scatter x1, waiting for transfers between devices, per_device(): lax.psum_scatter((jnp.dot(gate_grad, w_gate, preferred_element_type=jnp.f...  71.7 us
    unnamed x6, waiting for transfers between devices  34.8 us
    all_gather x1, blocking collectives, per_device(): lax.all_gather(layer_out, 'tensor', axis=1, tiled=True)  25.3 us
    all_gather x1, blocking collectives, per_device(): lax.all_gather(lengths, 'dp', axis=0, tiled=True)  21.8 us
    all_gather x1, blocking collectives, per_device(): lax.all_gather(resid_mid, 'tensor', axis=1, tiled=True)  20.3 us
  transfers between devices with their start and end apart: 6, of which 3 were waited for; matrix products, arithmetic and copies ran while one was open for 6% of the time, Pallas kernels for 0%

commit v1 on v0

v1 whole, which is shorter than its diff:
```python
import jax
import jax.numpy as jnp
from jax import lax
from jax.experimental import pallas as pl
from jax.experimental.pallas import tpu as pltpu
from jax.sharding import PartitionSpec as P

D = 5120
SLOT = 4
EPS = 1e-06
CE_WEIGHT = 0.5
LOSS_SCALE = 4096.0

BLOCK = 640
SLICE = 1280
CHIPS = 16
F32 = jnp.float32
BF16 = jnp.bfloat16
VMEM_LIMIT = 52 * 1024 * 1024
GRADS_VMEM = 20 * 1024 * 1024


def contract_cols(left, right):
    return lax.dot_general(left, right, (((1,), (1,)), ((), ())), preferred_element_type=F32)


def wrap(v, size):
    return jnp.where(v >= size, v - size, v)


def ring_bits(v):
    high = v // 2
    return v % 2 + high - 2 * (v % 2) * high, high


class Spot:
    def __init__(self):
        self.d = lax.axis_index("dp")
        self.z = lax.axis_index("tensor")
        self.chip = lax.div(self.d, 2)
        self.c = self.d - 2 * self.chip
        self.y = lax.div(self.chip, 4)
        self.x = self.chip - 4 * self.y
        c, other = self.c, 1 - self.c
        xv, yv = lax.div(self.x, 2), lax.div(self.y, 2)
        x_low, y_low = self.x - 2 * xv, self.y - 2 * yv
        xu, yu = x_low + xv - 2 * x_low * xv, y_low + yv - 2 * y_low * yv
        x_near, y_near = self.x + 1 - 2 * x_low, self.y + 1 - 2 * y_low
        x_far, y_far = 3 - self.x, 3 - self.y
        self.half = lax.div(self.z, 4)
        self.z_low = self.z - 4 * self.half
        bits = (xu, yu, xv, yv)
        moved = (x_near, y_near, x_far, y_far)
        self.own_bits = [bits[i] * other + bits[(i + 2) % 4] * c for i in range(4)]
        self.sib_bits = [bits[i] * c + bits[(i + 2) % 4] * other for i in range(4)]
        self.moved = [moved[i] * other + moved[(i + 2) % 4] * c for i in range(4)]
        self.own_base = [self.bases(self.own_bits, kk) for kk in range(2)]
        self.sib_base = [self.bases(self.sib_bits, kk) for kk in range(2)]

    def bases(self, bits, kk):
        out = [jnp.int32(0)]
        for s in range(4):
            out.append(out[-1] + bits[(kk + s) % 4] * (8 >> s))
        return out

    def bit(self, kk, s):
        return self.own_bits[(kk + s) % 4]

    def sib_bit(self, kk, s):
        return self.sib_bits[(kk + s) % 4]

    def place(self, kk):
        return self.own_base[kk][4]

    def partner(self, kk, s):
        i = (kk + s) % 4
        chip = self.y * 4 + self.moved[i] if i % 2 == 0 else self.moved[i] * 4 + self.x
        return (chip * 2 + self.c, self.z)

    def diagonal(self, kk, s):
        i, j = (kk + s) % 4, (kk + s + 1) % 4
        x, y = (self.moved[i], self.moved[j]) if i % 2 == 0 else (self.moved[j], self.moved[i])
        return ((y * 4 + x) * 2 + self.c, self.z)

    def sibling(self):
        return (self.chip * 2 + 1 - self.c, self.z)

    def column_peer(self, i):
        core = self.c if i % 2 == 0 else 1 - self.c
        return (self.chip * 2 + core, wrap(self.z + i // 2, 8) if i > 1 else self.z)


def greet(spot):
    barrier = pltpu.get_barrier_semaphore()
    for i in range(1, 16):
        pl.semaphore_signal(barrier, inc=1, device_id=spot.column_peer(i), device_id_type=pl.DeviceIdType.MESH)

    def body(j, carry):
        chip = wrap(spot.chip + j, CHIPS)
        for core in range(2):
            pl.semaphore_signal(
                barrier, inc=1, device_id=(chip * 2 + core, spot.z), device_id_type=pl.DeviceIdType.MESH
            )
        return carry

    lax.fori_loop(1, CHIPS, body, 0)


def greeted():
    pl.semaphore_wait(pltpu.get_barrier_semaphore(), 45)


def remote(src, dst, send_sem, recv_sem, target):
    return pltpu.make_async_remote_copy(
        src_ref=src,
        dst_ref=dst,
        send_sem=send_sem,
        recv_sem=recv_sem,
        device_id=target,
        device_id_type=pl.DeviceIdType.MESH,
    )


def row_scale(raw, core):
    total = jnp.zeros((8, BLOCK), F32)
    for zb in range(8):
        part = raw[8 * core + zb].astype(F32)
        total = total + part * part
    return lax.rsqrt(jnp.sum(total, axis=1, keepdims=True) / D + EPS)


def wait_bytes(ref, sem):
    pltpu.make_async_copy(ref, ref, sem).wait()


class Gather:
    def __init__(self, spot, full, xy_send, xy_recv, sib_send, sib_recv):
        self.spot, self.full = spot, full
        self.xy_send, self.xy_recv, self.sib_send, self.sib_recv = xy_send, xy_recv, sib_send, sib_recv

    def view(self, kk, off, n, core=None):
        core = self.spot.c if core is None else core
        return self.full.at[2 * core + kk, pl.ds(off, n)]

    def send(self, kk, target, idx, off, n):
        view = self.view(kk, off, n)
        remote(view, view, self.xy_send.at[kk], self.xy_recv.at[kk, idx], target).start()

    def arrived(self, kk, idx, off, n):
        wait_bytes(self.view(kk, off, n), self.xy_recv.at[kk, idx])

    def pass_on(self, kk, idx, off, n):
        view = self.view(kk, off, n)
        remote(view, view, self.sib_send.at[kk], self.sib_recv.at[kk, idx], self.spot.sibling()).start()

    def step(self, stage, kk):
        spot = self.spot
        flip = [(8 >> s) * (1 - 2 * spot.bit(kk, s)) for s in range(4)]
        own, four = spot.place(kk), spot.own_base[kk][2]
        if stage == 0:
            self.send(kk, spot.diagonal(kk, 2), 2, own, 1)
            self.send(kk, spot.partner(kk, 3), 0, own, 1)
            self.send(kk, spot.partner(kk, 2), 1, own, 1)
        elif stage == 1:
            self.arrived(kk, 0, own + flip[3], 1)
            self.arrived(kk, 1, own + flip[2], 1)
            self.arrived(kk, 2, own + flip[2] + flip[3], 1)
            self.send(kk, spot.partner(kk, 1), 3, four, 2)
            self.send(kk, spot.partner(kk, 1), 4, four + 2, 2)
            self.send(kk, spot.partner(kk, 0), 5, four, 4)
            self.pass_on(kk, 0, four, 4)
        elif stage == 2:
            new = four + flip[1]
            for i in range(2):
                self.arrived(kk, 3 + i, new + 2 * i, 2)
                self.send(kk, spot.partner(kk, 0), 6 + i, new + 2 * i, 2)
            self.pass_on(kk, 1, new, 4)
        elif stage == 3:
            new = four + flip[0]
            self.arrived(kk, 5, new, 4)
            self.pass_on(kk, 2, new, 4)
            new = new + flip[1]
            for i in range(2):
                self.arrived(kk, 6 + i, new + 2 * i, 2)
                self.pass_on(kk, 3 + i, new + 2 * i, 2)
        else:
            other = 1 - spot.c
            four = spot.sib_base[kk][2]
            over_1 = four + 4 * (1 - 2 * spot.sib_bit(kk, 1))
            over_0 = 8 * (1 - 2 * spot.sib_bit(kk, 0))
            last = over_1 + over_0
            pieces = ((four, 4), (over_1, 4), (four + over_0, 4), (last, 2), (last + 2, 2))
            for idx, (off, n) in enumerate(pieces):
                wait_bytes(self.view(kk, off, n, other), self.sib_recv.at[kk, idx])

    def finish(self):
        for kk in range(2):
            wait_bytes(self.full.at[kk, pl.ds(0, 15)], self.xy_send.at[kk])
            wait_bytes(self.full.at[kk], self.sib_send.at[kk])


def block_place(k, chip):
    xu, xv = ring_bits(chip % 4)
    yu, yv = ring_bits(chip // 4)
    bits = (xu, yu, xv, yv)
    return sum(bits[(k + s) % 4] * (8 >> s) for s in range(4))


def slice_columns(kk, core):
    return pl.ds(pl.multiple_of((2 * core + kk) * SLICE, SLICE), SLICE)


def lay_out(full, out, kk, core):
    for chip in range(CHIPS):
        low, high = block_place(kk, chip), block_place(2 + kk, chip)
        out[16 * chip : 16 * chip + 16, slice_columns(kk, core)] = full[2 * core + kk, low + (high - low) * core]


REDUCE_SCRATCH = [
    pltpu.VMEM((4, 16, 16, SLICE), BF16),
    pltpu.VMEM((2, 16, 16, SLICE), BF16),
    pltpu.VMEM((2, 15, 16, SLICE), BF16),
    pltpu.VMEM((8, 8, BLOCK), BF16),
    pltpu.VMEM((8, 8, BLOCK), BF16),
    pltpu.VMEM((2, 1, 128), F32),
    pltpu.VMEM((9, 1, 128), F32),
    pltpu.SemaphoreType.DMA((2,)),
    pltpu.SemaphoreType.DMA((2, 2)),
    pltpu.SemaphoreType.DMA((2,)),
    pltpu.SemaphoreType.DMA((2, 7)),
    pltpu.SemaphoreType.DMA((6,)),
]


class Reduce:
    def __init__(self, spot, scratch):
        self.spot = spot
        (
            self.partial,
            self.from_sib,
            self.from_xy,
            self.to_col,
            self.from_col,
            self.inner_to,
            self.inner_from,
            self.sib_send,
            self.sib_recv,
            self.xy_send,
            self.xy_recv,
            self.col_sems,
        ) = scratch

    def sib_copy(self, kk, sub, core, bit):
        half = (1 - bit) if sub == 0 else bit
        return remote(
            self.partial.at[2 * core + kk, pl.ds(half * 8, 8)],
            self.from_sib.at[kk, pl.ds(half * 8, 8)],
            self.sib_send.at[kk],
            self.sib_recv.at[kk, sub],
            self.spot.sibling(),
        )

    def start(self, kk, sub):
        self.sib_copy(kk, sub, 1 - self.spot.c, self.spot.sib_bit(kk, 0)).start()

    def from_sibling(self, kk, sub):
        self.sib_copy(kk, sub, self.spot.c, self.spot.bit(kk, 0)).wait_recv()

    def add(self, kk, off, ref, ref_off, n):
        k = 2 * self.spot.c + kk

        def body(i, carry):
            self.partial[k, off + i] = self.partial[k, off + i] + ref[kk, ref_off + i]
            return carry

        if n == 1:
            body(0, 0)
        else:
            lax.fori_loop(0, n, body, 0)

    def plan(self, kk, s):
        n = 8 >> s
        landing = 16 - 2 * n
        bit = self.spot.bit(kk, s)
        gone = self.spot.own_base[kk][s] + (1 - bit) * n
        kept = self.spot.own_base[kk][s] + bit * n
        half = n // 2
        after = self.spot.bit(kk, s + 1)
        pieces = []
        for sub in range(2):
            shift = ((1 - after) if sub == 0 else after) * half
            pieces.append((gone + shift, kept + shift, landing + sub * half, half, 2 * s + sub))
        return pieces

    def xy_copy(self, kk, s, piece):
        gone, _, landing, n, idx = piece
        return remote(
            self.partial.at[2 * self.spot.c + kk, pl.ds(gone, n)],
            self.from_xy.at[kk, pl.ds(landing, n)],
            self.xy_send.at[kk],
            self.xy_recv.at[kk, idx],
            self.spot.partner(kk, s),
        )

    def xy_start(self, kk, s, piece):
        self.xy_copy(kk, s, piece).start()

    def plane(self, beside=None):
        beside = beside or {}
        spot = self.spot
        for kk in range(2):
            self.from_sibling(kk, 0)
            for piece in self.plan(kk, 0):
                self.add(kk, piece[0], self.from_sib, piece[0], piece[3])
                self.xy_start(kk, 0, piece)
        for kk in range(2):
            self.from_sibling(kk, 1)
            self.add(kk, spot.bit(kk, 0) * 8, self.from_sib, spot.bit(kk, 0) * 8, 8)
        for work in beside.get(-1, ()):
            work()
        for kk in range(2):
            piece = self.plan(kk, 0)[0]
            self.xy_copy(kk, 0, piece).wait_recv()
            self.add(kk, piece[1], self.from_xy, piece[2], piece[3])
            for follow in self.plan(kk, 1):
                self.xy_start(kk, 1, follow)
        for kk in range(2):
            piece = self.plan(kk, 0)[1]
            self.xy_copy(kk, 0, piece).wait_recv()
            self.add(kk, piece[1], self.from_xy, piece[2], piece[3])
        for work in beside.get(0, ()):
            work()
        places = []
        for kk in range(2):
            own = spot.place(kk)
            by_2 = own + 2 * (1 - 2 * spot.bit(kk, 2))
            flip_3 = 1 - 2 * spot.bit(kk, 3)
            places.append((own, by_2, flip_3))
        for kk in range(2):
            piece = self.plan(kk, 1)[0]
            own, by_2, flip_3 = places[kk]
            self.xy_copy(kk, 1, piece).wait_recv()
            self.add(kk, piece[1], self.from_xy, piece[2], piece[3])
            self.tail_copy(kk, by_2 + flip_3, 2, spot.diagonal(kk, 2)).start()
            self.tail_copy(kk, by_2, 0, spot.partner(kk, 2)).start()
        for kk in range(2):
            piece = self.plan(kk, 1)[1]
            own, by_2, flip_3 = places[kk]
            self.xy_copy(kk, 1, piece).wait_recv()
            self.add(kk, piece[1], self.from_xy, piece[2], piece[3])
            self.tail_copy(kk, own + flip_3, 1, spot.partner(kk, 3)).start()
        for work in beside.get(1, ()):
            work()
        sums = []
        for kk in range(2):
            total = self.partial[2 * spot.c + kk, places[kk][0]].astype(F32)
            for i in range(3):
                self.tail_copy(kk, places[kk][0], i, spot.sibling()).wait_recv()
                total = total + self.from_xy[kk, 12 + i].astype(F32)
            sums.append(total)
        return sums

    def tail_copy(self, kk, block, i, target):
        return remote(
            self.partial.at[2 * self.spot.c + kk, pl.ds(block, 1)],
            self.from_xy.at[kk, pl.ds(12 + i, 1)],
            self.xy_send.at[kk],
            self.xy_recv.at[kk, 4 + i],
            target,
        )

    def column(self, sums, raw, gain, scale, beside=()):
        spot = self.spot
        for kk in range(2):
            for j in range(2):
                for core in range(2):
                    part = sums[kk][8 * core : 8 * core + 8, j * BLOCK : (j + 1) * BLOCK]
                    self.to_col[2 * (2 * kk + j) + core] = part.astype(BF16)
        row = lax.broadcasted_iota(jnp.int32, (8, 128), 0)
        diagonal = row == lax.broadcasted_iota(jnp.int32, (8, 128), 1)
        for core in range(2):
            total = jnp.zeros((8, BLOCK), F32)
            for kk in range(2):
                for j in range(2):
                    zb = 4 * spot.c + 2 * kk + j
                    part = sums[kk][8 * core : 8 * core + 8, j * BLOCK : (j + 1) * BLOCK]
                    total = total + raw[8 * core + zb].astype(F32) * gain[zb] * part
            inner = jnp.where(diagonal, jnp.sum(total, axis=1, keepdims=True), 0.0)
            self.inner_to[core] = jnp.sum(inner, axis=0, keepdims=True)
        to_sibling = remote(
            self.inner_to.at[1 - spot.c],
            self.inner_from.at[8],
            self.col_sems.at[4],
            self.col_sems.at[5],
            spot.sibling(),
        )
        to_sibling.start()
        for i in range(8):
            zdst = 4 * spot.c + i // 2
            mine = jnp.logical_and(zdst == spot.z, spot.c == i % 2)

            @pl.when(jnp.logical_not(mine))
            def _(i=i, zdst=zdst):
                remote(
                    self.to_col.at[i],
                    self.from_col.at[spot.z],
                    self.col_sems.at[0],
                    self.col_sems.at[1],
                    (spot.chip * 2 + i % 2, zdst),
                ).start()

            @pl.when(mine)
            def _(i=i):
                self.from_col[spot.z] = self.to_col[i]

        to_sibling.wait_recv()
        self.inner_from[0] = self.inner_to[spot.c] + self.inner_from[8]
        for i in range(1, 8):
            remote(
                self.inner_from.at[0],
                self.inner_from.at[i],
                self.col_sems.at[2],
                self.col_sems.at[3],
                spot.column_peer(2 * i),
            ).start()
        for work in beside:
            work()
        own = raw[8 * spot.c + spot.z].astype(F32)
        own_gain = gain[spot.z]
        wait_column(spot, self.from_col, self.col_sems.at[1])
        grad = jnp.zeros((8, BLOCK), F32)
        for zsrc in range(8):
            grad = grad + self.from_col[zsrc].astype(F32)
        wait_bytes(self.inner_from.at[pl.ds(1, 7)], self.col_sems.at[3])
        inner = jnp.zeros((1, 128), F32)
        for i in range(8):
            inner = inner + self.inner_from[i]
        inner = jnp.sum(jnp.where(diagonal, inner, 0.0), axis=1, keepdims=True) / D
        return scale * own_gain * grad - own * (scale * scale * scale) * inner

    def finish(self):
        for kk in range(2):
            wait_bytes(self.partial.at[kk], self.sib_send.at[kk])
            wait_bytes(self.partial.at[kk, pl.ds(0, 15)], self.xy_send.at[kk])
        wait_column(self.spot, self.to_col, self.col_sems.at[0])
        wait_bytes(self.inner_from.at[pl.ds(1, 7)], self.col_sems.at[2])
        wait_bytes(self.inner_from.at[pl.ds(8, 1)], self.col_sems.at[4])


def wait_column(spot, ref, sem):
    own = spot.half == spot.c

    @pl.when(own)
    def _():
        wait_bytes(ref.at[pl.ds(0, 7)], sem)

    @pl.when(jnp.logical_not(own))
    def _():
        wait_bytes(ref, sem)


def program(
    layer_out,
    resid_mid,
    final_gain,
    mlp_gain,
    teacher_in,
    assign,
    lengths,
    token_ids,
    head_hbm,
    gate_hbm,
    up_hbm,
    down_hbm,
    grad_first,
    grad_second,
    final_rows,
    normed,
    grad_rows,
    dlog_t,
    hidden_t,
    activated_t,
    head,
    w_gate_up,
    w_down,
    dlog,
    dlog_turned,
    hidden_turned,
    raw_out,
    raw_mid,
    full_out,
    full_mid,
    full_grad,
    packed,
    got,
    logits_ref,
    gate_up_pre,
    act_grad,
    first,
    second,
    stats_pad,
    own_b,
    own_from,
    scale_ref,
    load_sem,
    raw_sems,
    plane_sems,
    stat_sems,
    own_sems,
    xy_send,
    xy_recv,
    sib_send,
    sib_recv,
    *scratch,
):
    spot = Spot()
    c, other = spot.c, 1 - spot.c
    loads = [
        pltpu.make_async_copy(src, dst, load_sem.at[i])
        for i, (src, dst) in enumerate(
            (
                (head_hbm, head),
                (gate_hbm, w_gate_up.at[pl.ds(0, 64)]),
                (up_hbm, w_gate_up.at[pl.ds(64, 64)]),
                (down_hbm, w_down),
            )
        )
    ]
    for load in loads:
        load.start()
    reduces = [Reduce(spot, scratch[: len(REDUCE_SCRATCH)]), Reduce(spot, scratch[len(REDUCE_SCRATCH) :])]
    gathers = [
        Gather(spot, full, xy_send.at[a], xy_recv.at[a], sib_send.at[a], sib_recv.at[a])
        for a, full in enumerate((full_out, full_mid, full_grad))
    ]
    gather_out, gather_mid, gather_grad = gathers

    greet(spot)
    mine = 8 * c + spot.z
    raw_out[mine] = layer_out[...]
    raw_mid[mine] = resid_mid[...]

    row = lax.broadcasted_iota(jnp.int32, (8, 128), 0)
    lane = lax.broadcasted_iota(jnp.int32, (8, 128), 1)

    def by_row(values):
        out = jnp.zeros((8, 128), jnp.int32)
        for r, value in enumerate(values):
            out = jnp.where(row == r, value, out)
        return out

    order = by_row([assign[0, r] for r in range(8)])[:, 0:1]
    ids = by_row([token_ids[r] for r in range(8)])
    slots = by_row([lengths[0, r // SLOT] for r in range(8)])
    live = (lax.rem(row, SLOT) < slots).astype(jnp.int32)
    picked = jnp.zeros((8, teacher_in.shape[1]), F32)
    for r in range(8):
        picked = picked + jnp.where(order == r, teacher_in[r : r + 1, :].astype(F32), 0.0)
    picked = picked.astype(BF16)
    digits = jnp.where(lane == 0, ids >> 12, jnp.where(lane == 1, (ids >> 6) & 63, ids & 63))
    digits = jnp.where(lane == 3, live, digits)
    extras = digits.astype(F32).astype(BF16)
    for peer in range(32):
        packed[peer, :, 0:384] = picked[:, peer * 384 : (peer + 1) * 384]
        packed[peer, :, 384:512] = extras
    got[spot.d] = packed[spot.d]
    greeted()

    def send_raw(a, own, raw):
        for i in range(1, 8):
            remote(own, raw.at[mine], raw_sems.at[a, 0], raw_sems.at[a, 1], spot.column_peer(2 * i)).start()

    def pass_raw(a, raw):
        wait_bytes(raw.at[pl.ds(0, 7)], raw_sems.at[a, 1])
        rows = raw.at[pl.ds(8 * c, 8)]
        remote(rows, rows, raw_sems.at[a, 2], raw_sems.at[a, 3], spot.sibling()).start()

    def plane_start(i, carry):
        peer = wrap(spot.d + i, 32)
        remote(packed.at[peer], got.at[spot.d], plane_sems.at[0], plane_sems.at[1], (peer, spot.z)).start()
        return carry

    def normalise(a, raw, full, gain):
        wait_bytes(raw.at[pl.ds(0, 8)], raw_sems.at[a, 3])
        scales = [row_scale(raw, core) for core in range(2)]
        for kk in range(2):
            place = spot.place(kk)
            for j in range(2):
                zb = 4 * c + 2 * kk + j
                rows = jnp.concatenate(
                    [raw[8 * core + zb].astype(F32) * scales[core] * gain[zb] for core in range(2)], axis=0
                )
                full[2 * c + kk, place, :, j * BLOCK : (j + 1) * BLOCK] = rows.astype(BF16)
        for core in range(2):
            scale_ref[a, core] = jnp.broadcast_to(scales[core], (8, 128))

    def both(gather, stage):
        for kk in range(2):
            gather.step(stage, kk)

    send_raw(0, layer_out, raw_out)
    lax.fori_loop(1, 32, plane_start, 0)
    send_raw(1, resid_mid, raw_mid)
    pass_raw(0, raw_out)
    normalise(0, raw_out, full_out, final_gain)
    both(gather_out, 0)
    pass_raw(1, raw_mid)
    both(gather_out, 1)
    normalise(1, raw_mid, full_mid, mlp_gain)
    both(gather_out, 2)
    both(gather_out, 3)
    both(gather_mid, 0)

    def products(left, right, out, core, kks=(0, 1)):
        for kk in kks:
            columns = slice_columns(kk, core)
            out[...] += contract_cols(left[:, columns], right[:, columns])

    for kk in range(2):
        lay_out(full_out, final_rows, kk, c)
    loads[0].wait()
    logits_ref[...] = jnp.zeros_like(logits_ref)
    products(final_rows, head, logits_ref, c)
    both(gather_mid, 1)
    both(gather_out, 4)
    for kk in range(2):
        lay_out(full_out, final_rows, kk, other)
    products(final_rows, head, logits_ref, other)
    both(gather_mid, 2)

    wait_bytes(got.at[pl.ds(0, 31)], plane_sems.at[1])
    logits = logits_ref[...]
    packed_rows = got[...].astype(F32).reshape(256, 512)
    teacher = packed_rows[:, :384]
    digits = packed_rows[:, 384:]
    local_max = jnp.max(logits, axis=1, keepdims=True)
    expd = jnp.exp(logits - local_max)
    total = jnp.sum(expd, axis=1, keepdims=True)
    moment = jnp.sum(expd * (logits - teacher), axis=1, keepdims=True)
    lanes = lax.broadcasted_iota(jnp.int32, (256, 128), 1)
    columns = jnp.where(lanes == 0, local_max, jnp.where(lanes == 1, total, moment))
    first[0] = jnp.transpose(columns)[0:4]
    for i in range(1, 16):
        remote(first.at[0], first.at[i], stat_sems.at[0], stat_sems.at[1], spot.column_peer(i)).start()
    both(gather_mid, 3)

    def combine(ref):
        top = ref[0, 0:1]
        for i in range(1, 16):
            top = jnp.maximum(top, ref[i, 0:1])
        total = jnp.zeros_like(top)
        moment = jnp.zeros_like(top)
        for i in range(16):
            weight = jnp.exp(ref[i, 0:1] - top)
            total = total + ref[i, 1:2] * weight
            moment = moment + ref[i, 2:3] * weight
        return jnp.concatenate([top, total, moment, moment], axis=0)

    wait_bytes(first.at[pl.ds(1, 15)], stat_sems.at[1])
    second[0] = combine(first)
    for i in range(1, 16):
        target = (wrap(spot.chip + i, CHIPS) * 2 + c, spot.z)
        remote(second.at[0], second.at[i], stat_sems.at[2], stat_sems.at[3], target).start()
    ids_all = (digits[:, 0:1] * 4096 + digits[:, 1:2] * 64 + digits[:, 2:3]).astype(jnp.int32)
    live_mask = digits[:, 3:4]
    token_weight = live_mask * (LOSS_SCALE / jnp.sum(live_mask, axis=0, keepdims=True))
    vocab_start = (spot.z * 32 + spot.d) * 384
    vocab = lax.broadcasted_iota(jnp.int32, (256, 384), 1)
    target = (ids_all - vocab_start == vocab).astype(F32)
    stats_pad[...] = jnp.zeros_like(stats_pad)
    wait_bytes(second.at[pl.ds(1, 15)], stat_sems.at[3])
    stats_pad[0:4] = combine(second)
    columns = jnp.transpose(stats_pad[...])
    global_max, totals, moments = columns[:, 0:1], columns[:, 1:2], columns[:, 2:3]
    probs_all = jnp.exp(logits - global_max) / totals
    dlogits = token_weight * (
        probs_all * (logits - teacher - moments / totals + CE_WEIGHT) - CE_WEIGHT * target
    )
    def turn(rows, out):
        for k in range(4):
            for chip in range(CHIPS):
                place = 16 * block_place(k, chip)
                out[k, place : place + 16, :] = rows[16 * chip : 16 * chip + 16]

    def spread(reduce, kk, core, half, left, right):
        k = 2 * core + kk
        rows = left[k, pl.ds(pl.multiple_of(half * 128, 128), 128)]
        part = jnp.dot(rows, right[:, slice_columns(kk, core)], preferred_element_type=F32).astype(BF16)
        reduce.partial[k, pl.ds(half * 8, 8)] = part.reshape(8, 16, SLICE)

    def send_partial(reduce, left, right):
        for sub in range(2):
            for kk in range(2):
                bit = spot.sib_bit(kk, 0)
                spread(reduce, kk, other, (1 - bit) if sub == 0 else bit, left, right)
                reduce.start(kk, sub)
        for sub in range(2):
            for kk in range(2):
                bit = spot.bit(kk, 0)
                spread(reduce, kk, c, (1 - bit) if sub == 0 else bit, left, right)

    dlog_b = dlogits.astype(BF16)
    turn(dlog_b, dlog_turned)
    dlog[...] = dlog_b

    def mid_rows(core):
        for kk in range(2):
            lay_out(full_mid, normed, kk, core)

    def mid_first():
        for load in loads[1:]:
            load.wait()
        gate_up_pre[...] = jnp.zeros_like(gate_up_pre)
        act_grad[...] = jnp.zeros_like(act_grad)
        mid_rows(c)
        products(w_gate_up, normed, gate_up_pre, c)

    def mid_second():
        both(gather_mid, 4)
        mid_rows(other)
        products(w_gate_up, normed, gate_up_pre, other)

    def activate():
        gate = gate_up_pre[0:64]
        activated_t[...] = (gate * jax.nn.sigmoid(gate) * gate_up_pre[64:128]).astype(BF16)

    def turn_dlog():
        dlog_t[...] = jnp.transpose(dlog[...].astype(F32)).astype(BF16)

    send_partial(reduces[0], dlog_turned, head)
    sums = reduces[0].plane({-1: [mid_first], 0: [mid_second], 1: [activate]})
    grad_out = reduces[0].column(sums, raw_out, final_gain, scale_ref[0, c][:, 0:1])
    own_b[...] = grad_out.astype(BF16)
    grad_first[...] = grad_out

    target_core = spot.half
    own_place = spot.z_low * 2 + c
    for zdst in range(8):
        mine = jnp.logical_and(spot.z == zdst, target_core == c)

        @pl.when(jnp.logical_not(mine))
        def _(zdst=zdst):
            target = (spot.chip * 2 + target_core, zdst)
            remote(own_b, own_from.at[own_place], own_sems.at[0], own_sems.at[1], target).start()

        @pl.when(mine)
        def _():
            own_from[own_place] = own_b[...]

    turn_dlog()
    wait_column(spot, own_from, own_sems.at[1])
    for kk in range(2):
        for j in range(2):
            zz = 2 * kk + j
            rows = jnp.concatenate([own_from[2 * zz + core].astype(F32) for core in range(2)], axis=0)
            full_grad[2 * c + kk, spot.place(kk), :, j * BLOCK : (j + 1) * BLOCK] = rows.astype(BF16)
        gather_grad.step(0, kk)
    for stage in range(1, 4):
        both(gather_grad, stage)
    for kk in range(2):
        lay_out(full_grad, grad_rows, kk, c)
    products(w_down, grad_rows, act_grad, c)
    both(gather_grad, 4)
    for kk in range(2):
        lay_out(full_grad, grad_rows, kk, other)
    products(w_down, grad_rows, act_grad, other)

    gate, up, act = gate_up_pre[0:64], gate_up_pre[64:128], act_grad[...]
    gate_sigmoid = jax.nn.sigmoid(gate)
    gate_grad = act * up * gate_sigmoid * (1.0 + gate * (1.0 - gate_sigmoid))
    both_grads = jnp.concatenate([gate_grad, act * gate * gate_sigmoid], axis=0)
    turn(jnp.transpose(both_grads).astype(BF16), hidden_turned)
    hidden_t[...] = both_grads.astype(BF16)
    send_partial(reduces[1], hidden_turned, w_gate_up)

    for a in range(2):
        wait_bytes(raw_out.at[pl.ds(0, 7)], raw_sems.at[a, 0])
        wait_bytes(raw_out.at[pl.ds(0, 8)], raw_sems.at[a, 2])
    wait_bytes(got.at[pl.ds(0, 31)], plane_sems.at[0])
    wait_bytes(first.at[pl.ds(1, 15)], stat_sems.at[0])
    wait_bytes(second.at[pl.ds(1, 15)], stat_sems.at[2])
    for gather in gathers:
        gather.finish()
    reduces[0].finish()
    wait_column(spot, own_from, own_sems.at[0])

    sums = reduces[1].plane()
    grad_second[...] = reduces[1].column(sums, raw_mid, mlp_gain, scale_ref[1, c][:, 0:1])
    reduces[1].finish()


def weight_grads(
    grad_first,
    grad_second,
    dlog_t,
    hidden_t,
    activated_t,
    final_rows,
    normed,
    grad_rows,
    grad_resid,
    grad_head,
    grad_gate,
    grad_up,
    grad_down,
    head_rows,
    gate_up_rows,
    down_rows,
    sems,
):
    def product(left, right):
        return jnp.dot(left, right, preferred_element_type=F32).astype(BF16)

    def store(src, dst, idx):
        copy = pltpu.make_async_copy(src, dst, sems.at[idx])
        copy.start()
        return copy

    grad_resid[...] = (grad_first[...] + grad_second[...]).astype(BF16)
    stores = []
    for k in range(4):
        columns = slice(k * SLICE, (k + 1) * SLICE)
        place = pl.ds(k * SLICE, SLICE)
        head_rows[:, columns] = product(dlog_t[...], final_rows[:, columns])
        stores.append(store(head_rows.at[:, place], grad_head.at[:, place], k))
    for k in range(4):
        columns = slice(k * SLICE, (k + 1) * SLICE)
        gate_up_rows[:, columns] = product(hidden_t[...], normed[:, columns])
    stores.append(store(gate_up_rows.at[pl.ds(0, 64)], grad_gate, 4))
    stores.append(store(gate_up_rows.at[pl.ds(64, 64)], grad_up, 5))
    for k in range(4):
        columns = slice(k * SLICE, (k + 1) * SLICE)
        down_rows[:, columns] = product(activated_t[...], grad_rows[:, columns])
    stores.append(store(down_rows, grad_down, 6))
    for copy in stores:
        copy.wait()


def shape(dims, dtype):
    return jax.ShapeDtypeStruct(dims, dtype)


def per_device(
    layer_out,
    resid_mid,
    final_gain,
    mlp_gain,
    head_weight,
    w_gate,
    w_up,
    w_down,
    teacher_logits,
    assign,
    lengths,
    token_ids,
):
    final_gain = final_gain.reshape(8, 1, BLOCK)
    mlp_gain = mlp_gain.reshape(8, 1, BLOCK)
    vmem = pl.BlockSpec(memory_space=pltpu.VMEM)
    smem = pl.BlockSpec(memory_space=pltpu.SMEM)
    hbm = pl.BlockSpec(memory_space=pl.ANY)
    full = pltpu.VMEM((4, 16, 16, SLICE), BF16)
    rows = pltpu.VMEM((256, D), BF16)
    dma = pltpu.SemaphoreType.DMA
    shared = pl.pallas_call(
        program,
        out_shape=[
            pltpu.VMEM((8, BLOCK), F32),
            pltpu.VMEM((8, BLOCK), F32),
            rows,
            rows,
            rows,
            pltpu.VMEM((384, 256), BF16),
            pltpu.VMEM((128, 256), BF16),
            pltpu.VMEM((64, 256), BF16),
        ],
        in_specs=[vmem] * 5 + [smem] * 3 + [hbm] * 4,
        out_specs=[vmem] * 8,
        scratch_shapes=[
            pltpu.VMEM((384, D), BF16),
            pltpu.VMEM((128, D), BF16),
            pltpu.VMEM((64, D), BF16),
            pltpu.VMEM((256, 384), BF16),
            pltpu.VMEM((4, 256, 384), BF16),
            pltpu.VMEM((4, 256, 128), BF16),
            pltpu.VMEM((16, 8, BLOCK), BF16),
            pltpu.VMEM((16, 8, BLOCK), BF16),
            full,
            full,
            full,
            pltpu.VMEM((32, 8, 512), BF16),
            pltpu.VMEM((32, 8, 512), BF16),
            pltpu.VMEM((256, 384), F32),
            pltpu.VMEM((128, 256), F32),
            pltpu.VMEM((64, 256), F32),
            pltpu.VMEM((16, 4, 256), F32),
            pltpu.VMEM((16, 4, 256), F32),
            pltpu.VMEM((128, 256), F32),
            pltpu.VMEM((8, BLOCK), BF16),
            pltpu.VMEM((8, 8, BLOCK), BF16),
            pltpu.VMEM((2, 2, 8, 128), F32),
            dma((4,)),
            dma((2, 4)),
            dma((2,)),
            dma((4,)),
            dma((2,)),
            dma((3, 2)),
            dma((3, 2, 8)),
            dma((3, 2)),
            dma((3, 2, 5)),
        ]
        + REDUCE_SCRATCH
        + REDUCE_SCRATCH,
        compiler_params=pltpu.CompilerParams(
            collective_id=0, has_side_effects=True, vmem_limit_bytes=VMEM_LIMIT
        ),
        name="backward",
    )(
        layer_out,
        resid_mid,
        final_gain,
        mlp_gain,
        teacher_logits,
        assign,
        lengths,
        token_ids,
        head_weight,
        w_gate,
        w_up,
        w_down,
    )
    return pl.pallas_call(
        weight_grads,
        out_shape=[
            shape((8, BLOCK), BF16),
            shape(head_weight.shape, BF16),
            shape(w_gate.shape, BF16),
            shape(w_up.shape, BF16),
            shape(w_down.shape, BF16),
        ],
        in_specs=[vmem] * 8,
        out_specs=[vmem] + [hbm] * 4,
        scratch_shapes=[
            pltpu.VMEM((384, D), BF16),
            pltpu.VMEM((128, D), BF16),
            pltpu.VMEM((64, D), BF16),
            dma((7,)),
        ],
        compiler_params=pltpu.CompilerParams(vmem_limit_bytes=GRADS_VMEM),
        cost_estimate=pl.CostEstimate(flops=2 * 256 * 576 * D, bytes_accessed=2 * 576 * D, transcendentals=0),
        name="weight_grads",
    )(shared[0], shared[1], shared[5], shared[6], shared[7], shared[2], shared[3], shared[4])


def solution(mesh):
    return jax.shard_map(
        per_device,
        mesh=mesh,
        in_specs=(
            P("dp", "tensor"),
            P("dp", "tensor"),
            P(),
            P(),
            P(("tensor", "dp"), None),
            P(("tensor", "dp"), None),
            P(("tensor", "dp"), None),
            P(("tensor", "dp"), None),
            P("dp", "tensor"),
            P("dp", None),
            P("dp", None),
            P("dp"),
        ),
        out_specs=(
            P("dp", "tensor"),
            P(("tensor", "dp"), None),
            P(("tensor", "dp"), None),
            P(("tensor", "dp"), None),
            P(("tensor", "dp"), None),
        ),
        check_vma=False,
    )
```

time: 710 us -> 123 us (0.17); the launches traced: 702 us -> 123 us
  waiting for transfers between devices: 365 us -> 0 us
  blocking collectives: 240 us -> 0 us
  Pallas kernels: 0 us -> 123 us
  matrix products: 29.6 us -> 0 us
  starting transfers between devices: 20.6 us -> 0 us
  other arithmetic: 19.2 us -> 0 us
  between operations: 15.5 us -> 0.64 us
  local copies, waits for them, and re-layouts: 12.4 us -> 0 us
    psum x1 -> x0, waiting for transfers between devices: 258 us -> none  [per_device(): lax.psum(jnp.dot(dlog_b, head_weight, preferred_element_type=jnp.float32)...]
    pallas_call x0 -> x2, Pallas kernels: none -> 123 us  [the longest x1 119 us: per_device(): pl.pallas_call(program, out_shape=[pltpu.VMEM((8, BLOCK), F32), pltpu.VME...]
    psum x2 -> x0, blocking collectives: 84.8 us -> none  [the longest x1 72.7 us: per_device(): lax.psum((jnp.sum(expd, axis=1), jnp.sum(expd * (logits - teacher), axis=...]
    pmax x1 -> x0, blocking collectives: 76.9 us -> none  [per_device(): global_max = lax.pmax(local_max, ('dp', 'tensor'))]
    reduce_scatter x1 -> x0, waiting for transfers between devices: 71.7 us -> none  [per_device(): lax.psum_scatter((jnp.dot(gate_grad, w_gate, preferred_element_type=jnp.f...]
    all_gather x3 -> x0, blocking collectives: 67.4 us -> none  [the longest x1 25.3 us: per_device(): lax.all_gather(layer_out, 'tensor', axis=1, tiled=True)]
    unnamed x6 -> x0, waiting for transfers between devices: 34.8 us -> none
    dot_general x11 -> x0, matrix products: 29.6 us -> none  [the longest x4 10.8 us: contract_cols(): lax.dot_general(left, right, (((1,), (1,)), ((), ())), preferred_element_...]
  transfers between devices with their start and end apart: 6 -> 0, of which waited for: 3 -> 0; matrix products, arithmetic and copies ran while one was open for 6% -> 0% of each run, Pallas kernels for 0% -> 0%
where the time goes in v1:
time: 123 us
  Pallas kernels  123 us (100%)
    pallas_call x1, Pallas kernels, per_device(): pl.pallas_call(program, out_shape=[pltpu.VMEM((8, BLOCK), F32), pltpu.VME...  119 us
    pallas_call x1, Pallas kernels, per_device(): pl.pallas_call(weight_grads, out_shape=[shape((8, BLOCK), BF16), shape(he...  4.15 us

profile of v1, /device:TPU:1, one launch (start us, length us, event | category | flops | bytes accessed | tf_op | source)
XLA Modules:
  0.0 123.4 jit_solution(7492803505729155198)
XLA Ops:
  0.6 118.6 %backward.1 = (f32[8,640]{1,0:T(8,128)S(1)}, f32[8,640]{1,0:T(8,128)S(1)}, bf16[256,5120]{1,0:T(8,128)(2,1)S(1)}, bf16[256,5120]{1,0:T(8,128)(2,1)S(1)}, bf16[25...) custom-call(bf16[8,640]{1,0:T(8,128)(2,1)} %layer_out.1, ...), custom_call_target="tpu_custom_call" | custom-call | tf_op jit(solution)/shard_map/backward/pallas_call | solution.py:865
  119.2 4.2 %weight_grads.1 = (bf16[8,640]{1,0:T(8,128)(2,1)}, bf16[384,5120]{1,0:T(8,128)(2,1)}, bf16[64,5120]{1,0:T(8,128)(2,1)}, bf16[64,5120]{1,0:T(8,128)(2,1)}, bf16[64,5120]{1,0:T(8,128)(2,1)}) custom-call(f32[8,640]{1,0:T(8,128)S(1)} %get-tuple-element.13.grad_first, f32[8,640]{1,0:T(8,128)S(1)} %get-tuple-element.14.grad_second, ...), custom_call_target="tpu_custom_call" | custom-call | flops 1509949440 | bytes 5898240 | tf_op jit(solution)/shard_map/weight_grads/pallas_call | solution.py:932

commit v2 on v1

--- a/solution.py
+++ b/solution.py
@@ -53,47 +53,58 @@
         moved = (x_near, y_near, x_far, y_far)
         self.own_bits = [bits[i] * other + bits[(i + 2) % 4] * c for i in range(4)]
         self.sib_bits = [bits[i] * c + bits[(i + 2) % 4] * other for i in range(4)]
-        self.moved = [moved[i] * other + moved[(i + 2) % 4] * c for i in range(4)]
-        self.own_base = [self.bases(self.own_bits, kk) for kk in range(2)]
-        self.sib_base = [self.bases(self.sib_bits, kk) for kk in range(2)]
-
-    def bases(self, bits, kk):
-        out = [jnp.int32(0)]
-        for s in range(4):
-            out.append(out[-1] + bits[(kk + s) % 4] * (8 >> s))
-        return out
+        moved = [moved[i] * other + moved[(i + 2) % 4] * c for i in range(4)]
+        self.chips = [self.y * 4 + moved[i] if i % 2 == 0 else moved[i] * 4 + self.x for i in range(4)]
+        corner = []
+        for i in range(4):
+            j = (i + 1) % 4
+            corner.append(moved[j] * 4 + moved[i] if i % 2 == 0 else moved[i] * 4 + moved[j])
+        self.corners = corner
+
+    def pick(self, values, kk, s):
+        first, second = values[s % 4], values[(s + 1) % 4]
+        return first + (second - first) * kk
 
     def bit(self, kk, s):
-        return self.own_bits[(kk + s) % 4]
+        return self.pick(self.own_bits, kk, s)
 
     def sib_bit(self, kk, s):
-        return self.sib_bits[(kk + s) % 4]
+        return self.pick(self.sib_bits, kk, s)
+
+    def base(self, kk, s):
+        return sum((self.bit(kk, i) * (8 >> i) for i in range(s)), jnp.int32(0))
+
+    def sib_base(self, kk, s):
+        return sum((self.sib_bit(kk, i) * (8 >> i) for i in range(s)), jnp.int32(0))
 
     def place(self, kk):
-        return self.own_base[kk][4]
+        return self.base(kk, 4)
 
     def partner(self, kk, s):
-        i = (kk + s) % 4
-        chip = self.y * 4 + self.moved[i] if i % 2 == 0 else self.moved[i] * 4 + self.x
-        return (chip * 2 + self.c, self.z)
+        return (self.pick(self.chips, kk, s) * 2 + self.c, self.z)
 
     def diagonal(self, kk, s):
-        i, j = (kk + s) % 4, (kk + s + 1) % 4
-        x, y = (self.moved[i], self.moved[j]) if i % 2 == 0 else (self.moved[j], self.moved[i])
-        return ((y * 4 + x) * 2 + self.c, self.z)
+        return (self.pick(self.corners, kk, s) * 2 + self.c, self.z)
 
     def sibling(self):
         return (self.chip * 2 + 1 - self.c, self.z)
 
-    def column_peer(self, i):
-        core = self.c if i % 2 == 0 else 1 - self.c
-        return (self.chip * 2 + core, wrap(self.z + i // 2, 8) if i > 1 else self.z)
+    def column_peer(self, up, flip=0):
+        core = self.c if flip == 0 else 1 - self.c
+        return (self.chip * 2 + core, wrap(self.z + up, 8))
 
 
 def greet(spot):
     barrier = pltpu.get_barrier_semaphore()
-    for i in range(1, 16):
-        pl.semaphore_signal(barrier, inc=1, device_id=spot.column_peer(i), device_id_type=pl.DeviceIdType.MESH)
+    mesh = pl.DeviceIdType.MESH
+    pl.semaphore_signal(barrier, inc=1, device_id=spot.sibling(), device_id_type=mesh)
+
+    def column(up, carry):
+        for flip in range(2):
+            pl.semaphore_signal(barrier, inc=1, device_id=spot.column_peer(up, flip), device_id_type=mesh)
+        return carry
+
+    lax.fori_loop(1, 8, column, 0)
 
     def body(j, carry):
         chip = wrap(spot.chip + j, CHIPS)
@@ -129,6 +140,14 @@
     return lax.rsqrt(jnp.sum(total, axis=1, keepdims=True) / D + EPS)
 
 
+def loop(start, stop, body):
+    def step(i, carry):
+        body(i)
+        return carry
+
+    lax.fori_loop(start, stop, step, 0)
+
+
 def wait_bytes(ref, sem):
     pltpu.make_async_copy(ref, ref, sem).wait()
 
@@ -156,7 +175,7 @@
     def step(self, stage, kk):
         spot = self.spot
         flip = [(8 >> s) * (1 - 2 * spot.bit(kk, s)) for s in range(4)]
-        own, four = spot.place(kk), spot.own_base[kk][2]
+        own, four = spot.place(kk), spot.base(kk, 2)
         if stage == 0:
             self.send(kk, spot.diagonal(kk, 2), 2, own, 1)
             self.send(kk, spot.partner(kk, 3), 0, own, 1)
@@ -185,7 +204,7 @@
                 self.pass_on(kk, 3 + i, new + 2 * i, 2)
         else:
             other = 1 - spot.c
-            four = spot.sib_base[kk][2]
+            four = spot.sib_base(kk, 2)
             over_1 = four + 4 * (1 - 2 * spot.sib_bit(kk, 1))
             over_0 = 8 * (1 - 2 * spot.sib_bit(kk, 0))
             last = over_1 + over_0
@@ -211,9 +230,24 @@
 
 
 def lay_out(full, out, kk, core):
-    for chip in range(CHIPS):
-        low, high = block_place(kk, chip), block_place(2 + kk, chip)
-        out[16 * chip : 16 * chip + 16, slice_columns(kk, core)] = full[2 * core + kk, low + (high - low) * core]
+    along_x = []
+    for x in range(4):
+        low, high = block_place(kk, x), block_place(2 + kk, x)
+        along_x.append(low + (high - low) * core)
+
+    def row(y):
+        yv = jnp.where(y >= 2, 1, 0)
+        y_low = y - 2 * yv
+        yu = y_low + yv - 2 * y_low * yv
+        weights = [(8 >> ((1 - k) % 4), 8 >> ((3 - k) % 4)) for k in (kk, 2 + kk)]
+        place_u = weights[0][0] + (weights[1][0] - weights[0][0]) * core
+        place_v = weights[0][1] + (weights[1][1] - weights[0][1]) * core
+        along_y = yu * place_u + yv * place_v
+        for x in range(4):
+            rows = pl.ds(pl.multiple_of(64 * y + 16 * x, 16), 16)
+            out[rows, slice_columns(kk, core)] = full[2 * core + kk, along_y + along_x[x]]
+
+    loop(0, 4, row)
 
 
 REDUCE_SCRATCH = [
@@ -251,7 +285,7 @@
         ) = scratch
 
     def sib_copy(self, kk, sub, core, bit):
-        half = (1 - bit) if sub == 0 else bit
+        half = (1 - sub) * (1 - bit) + sub * bit
         return remote(
             self.partial.at[2 * core + kk, pl.ds(half * 8, 8)],
             self.from_sib.at[kk, pl.ds(half * 8, 8)],
@@ -282,8 +316,8 @@
         n = 8 >> s
         landing = 16 - 2 * n
         bit = self.spot.bit(kk, s)
-        gone = self.spot.own_base[kk][s] + (1 - bit) * n
-        kept = self.spot.own_base[kk][s] + bit * n
+        gone = self.spot.base(kk, s) + (1 - bit) * n
+        kept = self.spot.base(kk, s) + bit * n
         half = n // 2
         after = self.spot.bit(kk, s + 1)
         pieces = []
@@ -308,54 +342,56 @@
     def plane(self, beside=None):
         beside = beside or {}
         spot = self.spot
-        for kk in range(2):
+
+        def first(kk):
             self.from_sibling(kk, 0)
             for piece in self.plan(kk, 0):
                 self.add(kk, piece[0], self.from_sib, piece[0], piece[3])
                 self.xy_start(kk, 0, piece)
-        for kk in range(2):
+
+        def kept(kk):
             self.from_sibling(kk, 1)
             self.add(kk, spot.bit(kk, 0) * 8, self.from_sib, spot.bit(kk, 0) * 8, 8)
+
+        def arrive(kk, s, sub):
+            piece = self.plan(kk, s)[sub]
+            self.xy_copy(kk, s, piece).wait_recv()
+            self.add(kk, piece[1], self.from_xy, piece[2], piece[3])
+
+        def second(kk):
+            arrive(kk, 0, 0)
+            for follow in self.plan(kk, 1):
+                self.xy_start(kk, 1, follow)
+
+        def third(kk):
+            arrive(kk, 1, 0)
+            by_2 = spot.place(kk) + 2 * (1 - 2 * spot.bit(kk, 2))
+            self.tail_copy(kk, by_2 + 1 - 2 * spot.bit(kk, 3), 2, spot.diagonal(kk, 2)).start()
+            self.tail_copy(kk, by_2, 0, spot.partner(kk, 2)).start()
+
+        def fourth(kk):
+            arrive(kk, 1, 1)
+            own = spot.place(kk)
+            self.tail_copy(kk, own + 1 - 2 * spot.bit(kk, 3), 1, spot.partner(kk, 3)).start()
+
+        loop(0, 2, first)
+        loop(0, 2, kept)
         for work in beside.get(-1, ()):
             work()
-        for kk in range(2):
-            piece = self.plan(kk, 0)[0]
-            self.xy_copy(kk, 0, piece).wait_recv()
-            self.add(kk, piece[1], self.from_xy, piece[2], piece[3])
-            for follow in self.plan(kk, 1):
-                self.xy_start(kk, 1, follow)
-        for kk in range(2):
-            piece = self.plan(kk, 0)[1]
-            self.xy_copy(kk, 0, piece).wait_recv()
-            self.add(kk, piece[1], self.from_xy, piece[2], piece[3])
+        loop(0, 2, second)
+        loop(0, 2, lambda kk: arrive(kk, 0, 1))
         for work in beside.get(0, ()):
             work()
-        places = []
-        for kk in range(2):
-            own = spot.place(kk)
-            by_2 = own + 2 * (1 - 2 * spot.bit(kk, 2))
-            flip_3 = 1 - 2 * spot.bit(kk, 3)
-            places.append((own, by_2, flip_3))
-        for kk in range(2):
-            piece = self.plan(kk, 1)[0]
-            own, by_2, flip_3 = places[kk]
-            self.xy_copy(kk, 1, piece).wait_recv()
-            self.add(kk, piece[1], self.from_xy, piece[2], piece[3])
-            self.tail_copy(kk, by_2 + flip_3, 2, spot.diagonal(kk, 2)).start()
-            self.tail_copy(kk, by_2, 0, spot.partner(kk, 2)).start()
-        for kk in range(2):
-            piece = self.plan(kk, 1)[1]
-            own, by_2, flip_3 = places[kk]
-            self.xy_copy(kk, 1, piece).wait_recv()
-            self.add(kk, piece[1], self.from_xy, piece[2], piece[3])
-            self.tail_copy(kk, own + flip_3, 1, spot.partner(kk, 3)).start()
+        loop(0, 2, third)
+        loop(0, 2, fourth)
         for work in beside.get(1, ()):
             work()
+        places = [spot.place(kk) for kk in range(2)]
         sums = []
         for kk in range(2):
-            total = self.partial[2 * spot.c + kk, places[kk][0]].astype(F32)
+            total = self.partial[2 * spot.c + kk, places[kk]].astype(F32)
             for i in range(3):
-                self.tail_copy(kk, places[kk][0], i, spot.sibling()).wait_recv()
+                self.tail_copy(kk, places[kk], i, spot.sibling()).wait_recv()
                 total = total + self.from_xy[kk, 12 + i].astype(F32)
             sums.append(total)
         return sums
@@ -376,6 +412,27 @@
                 for core in range(2):
                     part = sums[kk][8 * core : 8 * core + 8, j * BLOCK : (j + 1) * BLOCK]
                     self.to_col[2 * (2 * kk + j) + core] = part.astype(BF16)
+
+        def to_column(zz):
+            zdst = 4 * spot.c + zz
+            for core in range(2):
+                mine = jnp.logical_and(zdst == spot.z, spot.c == core)
+
+                @pl.when(jnp.logical_not(mine))
+                def _(core=core):
+                    remote(
+                        self.to_col.at[2 * zz + core],
+                        self.from_col.at[spot.z],
+                        self.col_sems.at[0],
+                        self.col_sems.at[1],
+                        (spot.chip * 2 + core, zdst),
+                    ).start()
+
+                @pl.when(mine)
+                def _(core=core):
+                    self.from_col[spot.z] = self.to_col[2 * zz + core]
+
+        loop(0, 4, to_column)
         row = lax.broadcasted_iota(jnp.int32, (8, 128), 0)
         diagonal = row == lax.broadcasted_iota(jnp.int32, (8, 128), 1)
         for core in range(2):
@@ -395,34 +452,19 @@
             spot.sibling(),
         )
         to_sibling.start()
-        for i in range(8):
-            zdst = 4 * spot.c + i // 2
-            mine = jnp.logical_and(zdst == spot.z, spot.c == i % 2)
-
-            @pl.when(jnp.logical_not(mine))
-            def _(i=i, zdst=zdst):
-                remote(
-                    self.to_col.at[i],
-                    self.from_col.at[spot.z],
-                    self.col_sems.at[0],
-                    self.col_sems.at[1],
-                    (spot.chip * 2 + i % 2, zdst),
-                ).start()
-
-            @pl.when(mine)
-            def _(i=i):
-                self.from_col[spot.z] = self.to_col[i]
-
         to_sibling.wait_recv()
         self.inner_from[0] = self.inner_to[spot.c] + self.inner_from[8]
-        for i in range(1, 8):
-            remote(
+        loop(
+            1,
+            8,
+            lambda up: remote(
                 self.inner_from.at[0],
-                self.inner_from.at[i],
+                self.inner_from.at[up],
                 self.col_sems.at[2],
                 self.col_sems.at[3],
-                spot.column_peer(2 * i),
-            ).start()
+                spot.column_peer(up),
+            ).start(),
+        )
         for work in beside:
             work()
         own = raw[8 * spot.c + spot.z].astype(F32)
@@ -494,6 +536,7 @@
     packed,
     got,
     logits_ref,
+    diff_ref,
     gate_up_pre,
     act_grad,
     first,
@@ -540,35 +583,40 @@
     raw_out[mine] = layer_out[...]
     raw_mid[mine] = resid_mid[...]
 
-    row = lax.broadcasted_iota(jnp.int32, (8, 128), 0)
-    lane = lax.broadcasted_iota(jnp.int32, (8, 128), 1)
-
-    def by_row(values):
-        out = jnp.zeros((8, 128), jnp.int32)
-        for r, value in enumerate(values):
-            out = jnp.where(row == r, value, out)
-        return out
-
-    order = by_row([assign[0, r] for r in range(8)])[:, 0:1]
-    ids = by_row([token_ids[r] for r in range(8)])
-    slots = by_row([lengths[0, r // SLOT] for r in range(8)])
-    live = (lax.rem(row, SLOT) < slots).astype(jnp.int32)
-    picked = jnp.zeros((8, teacher_in.shape[1]), F32)
+    row = lax.broadcasted_iota(jnp.int32, (8, 1), 0)
+    order = jnp.zeros((8, 1), jnp.int32)
     for r in range(8):
-        picked = picked + jnp.where(order == r, teacher_in[r : r + 1, :].astype(F32), 0.0)
-    picked = picked.astype(BF16)
-    digits = jnp.where(lane == 0, ids >> 12, jnp.where(lane == 1, (ids >> 6) & 63, ids & 63))
-    digits = jnp.where(lane == 3, live, digits)
-    extras = digits.astype(F32).astype(BF16)
-    for peer in range(32):
-        packed[peer, :, 0:384] = picked[:, peer * 384 : (peer + 1) * 384]
-        packed[peer, :, 384:512] = extras
+        order = jnp.where(row == r, assign[0, r], order)
+
+    def pack(peer):
+        rows = teacher_in[:, pl.ds(pl.multiple_of(peer * 384, 384), 384)].astype(F32)
+        picked = jnp.zeros((8, 384), F32)
+        for r in range(8):
+            picked = picked + jnp.where(order == r, rows[r : r + 1, :], 0.0)
+        packed[peer] = picked.astype(BF16)
+
+    loop(0, 32, pack)
     got[spot.d] = packed[spot.d]
+
+    token = lax.broadcasted_iota(jnp.int32, (1, 256), 1)
+    own_ids = jnp.full((1, 256), -1, jnp.int32)
+    own_lengths = jnp.zeros((1, 256), jnp.int32)
+    for r in range(8):
+        here = token == 8 * spot.d + r
+        own_ids = jnp.where(here, token_ids[r], own_ids)
+        own_lengths = jnp.where(here, lengths[0, r // SLOT], own_lengths)
+    live = (lax.rem(token, SLOT) < own_lengths).astype(jnp.int32)
+    codes = jnp.where(own_ids >= 0, 2 * own_ids + live, 0).astype(F32)
     greeted()
 
     def send_raw(a, own, raw):
-        for i in range(1, 8):
-            remote(own, raw.at[mine], raw_sems.at[a, 0], raw_sems.at[a, 1], spot.column_peer(2 * i)).start()
+        loop(
+            1,
+            8,
+            lambda up: remote(
+                own, raw.at[mine], raw_sems.at[a, 0], raw_sems.at[a, 1], spot.column_peer(up)
+            ).start(),
+        )
 
     def pass_raw(a, raw):
         wait_bytes(raw.at[pl.ds(0, 7)], raw_sems.at[a, 1])
@@ -595,8 +643,7 @@
             scale_ref[a, core] = jnp.broadcast_to(scales[core], (8, 128))
 
     def both(gather, stage):
-        for kk in range(2):
-            gather.step(stage, kk)
+        loop(0, 2, lambda kk: gather.step(stage, kk))
 
     send_raw(0, layer_out, raw_out)
     lax.fori_loop(1, 32, plane_start, 0)
@@ -611,10 +658,12 @@
     both(gather_out, 3)
     both(gather_mid, 0)
 
-    def products(left, right, out, core, kks=(0, 1)):
-        for kk in kks:
+    def products(left, right, out, core):
+        def body(kk):
             columns = slice_columns(kk, core)
             out[...] += contract_cols(left[:, columns], right[:, columns])
+
+        loop(0, 2, body)
 
     for kk in range(2):
         lay_out(full_out, final_rows, kk, c)
@@ -630,21 +679,28 @@
 
     wait_bytes(got.at[pl.ds(0, 31)], plane_sems.at[1])
     logits = logits_ref[...]
-    packed_rows = got[...].astype(F32).reshape(256, 512)
-    teacher = packed_rows[:, :384]
-    digits = packed_rows[:, 384:]
+    diff = logits - got[...].astype(F32).reshape(256, 384)
     local_max = jnp.max(logits, axis=1, keepdims=True)
     expd = jnp.exp(logits - local_max)
     total = jnp.sum(expd, axis=1, keepdims=True)
-    moment = jnp.sum(expd * (logits - teacher), axis=1, keepdims=True)
+    moment = jnp.sum(expd * diff, axis=1, keepdims=True)
+    logits_ref[...] = expd
+    diff_ref[...] = diff
     lanes = lax.broadcasted_iota(jnp.int32, (256, 128), 1)
     columns = jnp.where(lanes == 0, local_max, jnp.where(lanes == 1, total, moment))
     first[0] = jnp.transpose(columns)[0:4]
-    for i in range(1, 16):
-        remote(first.at[0], first.at[i], stat_sems.at[0], stat_sems.at[1], spot.column_peer(i)).start()
+    first[0, 3:4] = codes
+    remote(first.at[0], first.at[1], stat_sems.at[0], stat_sems.at[1], spot.sibling()).start()
+
+    def to_column(up):
+        for flip in range(2):
+            target = spot.column_peer(up, flip)
+            remote(first.at[0], first.at[2 * up + flip], stat_sems.at[0], stat_sems.at[1], target).start()
+
+    loop(1, 8, to_column)
     both(gather_mid, 3)
 
-    def combine(ref):
+    def combine(ref, groups):
         top = ref[0, 0:1]
         for i in range(1, 16):
             top = jnp.maximum(top, ref[i, 0:1])
@@ -654,28 +710,31 @@
             weight = jnp.exp(ref[i, 0:1] - top)
             total = total + ref[i, 1:2] * weight
             moment = moment + ref[i, 2:3] * weight
-        return jnp.concatenate([top, total, moment, moment], axis=0)
+        return jnp.concatenate([top, total, moment, sum(ref[i, 3:4] for i in range(groups))], axis=0)
 
     wait_bytes(first.at[pl.ds(1, 15)], stat_sems.at[1])
-    second[0] = combine(first)
-    for i in range(1, 16):
+    second[0] = combine(first, 2)
+
+    def to_plane(i):
         target = (wrap(spot.chip + i, CHIPS) * 2 + c, spot.z)
         remote(second.at[0], second.at[i], stat_sems.at[2], stat_sems.at[3], target).start()
-    ids_all = (digits[:, 0:1] * 4096 + digits[:, 1:2] * 64 + digits[:, 2:3]).astype(jnp.int32)
-    live_mask = digits[:, 3:4]
-    token_weight = live_mask * (LOSS_SCALE / jnp.sum(live_mask, axis=0, keepdims=True))
-    vocab_start = (spot.z * 32 + spot.d) * 384
-    vocab = lax.broadcasted_iota(jnp.int32, (256, 384), 1)
-    target = (ids_all - vocab_start == vocab).astype(F32)
+
+    loop(1, CHIPS, to_plane)
+    vocab = lax.broadcasted_iota(jnp.int32, (256, 384), 1) + (spot.z * 32 + spot.d) * 384
     stats_pad[...] = jnp.zeros_like(stats_pad)
     wait_bytes(second.at[pl.ds(1, 15)], stat_sems.at[3])
-    stats_pad[0:4] = combine(second)
+    stats_pad[0:4] = combine(second, 16)
     columns = jnp.transpose(stats_pad[...])
     global_max, totals, moments = columns[:, 0:1], columns[:, 1:2], columns[:, 2:3]
-    probs_all = jnp.exp(logits - global_max) / totals
-    dlogits = token_weight * (
-        probs_all * (logits - teacher - moments / totals + CE_WEIGHT) - CE_WEIGHT * target
-    )
+    code = columns[:, 3:4].astype(jnp.int32)
+    ids_all = code >> 1
+    live_mask = (code - 2 * ids_all).astype(F32)
+    token_weight = live_mask * (LOSS_SCALE / jnp.sum(live_mask, axis=0, keepdims=True))
+    share = token_weight * (jnp.exp(local_max - global_max) / totals)
+    shift = CE_WEIGHT - moments / totals
+    dlogits = share * logits_ref[...] * (diff_ref[...] + shift)
+    dlogits = dlogits - jnp.where(ids_all == vocab, CE_WEIGHT * token_weight, 0.0)
+
     def turn(rows, out):
         for k in range(4):
             for chip in range(CHIPS):
@@ -689,15 +748,22 @@
         reduce.partial[k, pl.ds(half * 8, 8)] = part.reshape(8, 16, SLICE)
 
     def send_partial(reduce, left, right):
-        for sub in range(2):
-            for kk in range(2):
-                bit = spot.sib_bit(kk, 0)
-                spread(reduce, kk, other, (1 - bit) if sub == 0 else bit, left, right)
-                reduce.start(kk, sub)
-        for sub in range(2):
-            for kk in range(2):
-                bit = spot.bit(kk, 0)
-                spread(reduce, kk, c, (1 - bit) if sub == 0 else bit, left, right)
+
+        def to_sibling(i):
+            sub = jnp.where(i >= 2, 1, 0)
+            kk = i - 2 * sub
+            bit = spot.sib_bit(kk, 0)
+            spread(reduce, kk, other, (1 - sub) * (1 - bit) + sub * bit, left, right)
+            reduce.start(kk, sub)
+
+        def to_self(i):
+            sub = jnp.where(i >= 2, 1, 0)
+            kk = i - 2 * sub
+            bit = spot.bit(kk, 0)
+            spread(reduce, kk, c, (1 - sub) * (1 - bit) + sub * bit, left, right)
+
+        loop(0, 4, to_sibling)
+        loop(0, 4, to_self)
 
     dlog_b = dlogits.astype(BF16)
     turn(dlog_b, dlog_turned)
@@ -735,11 +801,12 @@
 
     target_core = spot.half
     own_place = spot.z_low * 2 + c
-    for zdst in range(8):
+
+    def own_to_column(zdst):
         mine = jnp.logical_and(spot.z == zdst, target_core == c)
 
         @pl.when(jnp.logical_not(mine))
-        def _(zdst=zdst):
+        def _():
             target = (spot.chip * 2 + target_core, zdst)
             remote(own_b, own_from.at[own_place], own_sems.at[0], own_sems.at[1], target).start()
 
@@ -747,6 +814,7 @@
         def _():
             own_from[own_place] = own_b[...]
 
+    loop(0, 8, own_to_column)
     turn_dlog()
     wait_column(spot, own_from, own_sems.at[1])
     for kk in range(2):
@@ -754,7 +822,7 @@
             zz = 2 * kk + j
             rows = jnp.concatenate([own_from[2 * zz + core].astype(F32) for core in range(2)], axis=0)
             full_grad[2 * c + kk, spot.place(kk), :, j * BLOCK : (j + 1) * BLOCK] = rows.astype(BF16)
-        gather_grad.step(0, kk)
+    both(gather_grad, 0)
     for stage in range(1, 4):
         both(gather_grad, stage)
     for kk in range(2):
@@ -811,29 +879,34 @@
     def product(left, right):
         return jnp.dot(left, right, preferred_element_type=F32).astype(BF16)
 
-    def store(src, dst, idx):
-        copy = pltpu.make_async_copy(src, dst, sems.at[idx])
-        copy.start()
-        return copy
-
     grad_resid[...] = (grad_first[...] + grad_second[...]).astype(BF16)
-    stores = []
-    for k in range(4):
-        columns = slice(k * SLICE, (k + 1) * SLICE)
-        place = pl.ds(k * SLICE, SLICE)
-        head_rows[:, columns] = product(dlog_t[...], final_rows[:, columns])
-        stores.append(store(head_rows.at[:, place], grad_head.at[:, place], k))
-    for k in range(4):
-        columns = slice(k * SLICE, (k + 1) * SLICE)
-        gate_up_rows[:, columns] = product(hidden_t[...], normed[:, columns])
-    stores.append(store(gate_up_rows.at[pl.ds(0, 64)], grad_gate, 4))
-    stores.append(store(gate_up_rows.at[pl.ds(64, 64)], grad_up, 5))
-    for k in range(4):
-        columns = slice(k * SLICE, (k + 1) * SLICE)
-        down_rows[:, columns] = product(activated_t[...], grad_rows[:, columns])
-    stores.append(store(down_rows, grad_down, 6))
-    for copy in stores:
-        copy.wait()
+
+    def copies(k):
+        place = pl.ds(pl.multiple_of(k * SLICE, SLICE), SLICE)
+        return [
+            pltpu.make_async_copy(head_rows.at[:, place], grad_head.at[:, place], sems.at[0, k]),
+            pltpu.make_async_copy(gate_up_rows.at[pl.ds(0, 64), place], grad_gate.at[:, place], sems.at[1, k]),
+            pltpu.make_async_copy(gate_up_rows.at[pl.ds(64, 64), place], grad_up.at[:, place], sems.at[2, k]),
+            pltpu.make_async_copy(down_rows.at[:, place], grad_down.at[:, place], sems.at[3, k]),
+        ]
+
+    def chunk(k):
+        place = pl.ds(pl.multiple_of(k * SLICE, SLICE), SLICE)
+        to_head, to_gate, to_up, to_down = copies(k)
+        head_rows[:, place] = product(dlog_t[...], final_rows[:, place])
+        to_head.start()
+        gate_up_rows[:, place] = product(hidden_t[...], normed[:, place])
+        to_gate.start()
+        to_up.start()
+        down_rows[:, place] = product(activated_t[...], grad_rows[:, place])
+        to_down.start()
+
+    def done(k):
+        for copy in copies(k):
+            copy.wait()
+
+    loop(0, 4, chunk)
+    loop(0, 4, done)
 
 
 def shape(dims, dtype):
@@ -888,8 +961,9 @@
             full,
             full,
             full,
-            pltpu.VMEM((32, 8, 512), BF16),
-            pltpu.VMEM((32, 8, 512), BF16),
+            pltpu.VMEM((32, 8, 384), BF16),
+            pltpu.VMEM((32, 8, 384), BF16),
+            pltpu.VMEM((256, 384), F32),
             pltpu.VMEM((256, 384), F32),
             pltpu.VMEM((128, 256), F32),
             pltpu.VMEM((64, 256), F32),
@@ -944,7 +1018,7 @@
             pltpu.VMEM((384, D), BF16),
             pltpu.VMEM((128, D), BF16),
             pltpu.VMEM((64, D), BF16),
-            dma((7,)),
+            dma((4, 4)),
         ],
         compiler_params=pltpu.CompilerParams(vmem_limit_bytes=GRADS_VMEM),
         cost_estimate=pl.CostEstimate(flops=2 * 256 * 576 * D, bytes_accessed=2 * 576 * D, transcendentals=0),

time: 123 us -> 124 us (level)
  no operation moved by 1% of the time
where the time goes in v2:
time: 124 us
  Pallas kernels  124 us (100%)
    pallas_call x1, Pallas kernels, per_device(): pl.pallas_call(program, out_shape=[pltpu.VMEM((8, BLOCK), F32), pltpu.VME...  120 us
    pallas_call x1, Pallas kernels, per_device(): pl.pallas_call(weight_grads, out_shape=[shape((8, BLOCK), BF16), shape(he...  4.13 us

profile of v2, /device:TPU:1, one launch (start us, length us, event | category | flops | bytes accessed | tf_op | source)
XLA Modules:
  0.0 124.3 jit_solution(7155880912663965361)
XLA Ops:
  0.6 119.5 %backward.1 = (f32[8,640]{1,0:T(8,128)S(1)}, f32[8,640]{1,0:T(8,128)S(1)}, bf16[256,5120]{1,0:T(8,128)(2,1)S(1)}, bf16[256,5120]{1,0:T(8,128)(2,1)S(1)}, bf16[25...) custom-call(bf16[8,640]{1,0:T(8,128)(2,1)} %layer_out.1, ...), custom_call_target="tpu_custom_call" | custom-call | tf_op jit(solution)/shard_map/backward/pallas_call | solution.py:938
  120.2 4.1 %weight_grads.1 = (bf16[8,640]{1,0:T(8,128)(2,1)}, bf16[384,5120]{1,0:T(8,128)(2,1)}, bf16[64,5120]{1,0:T(8,128)(2,1)}, bf16[64,5120]{1,0:T(8,128)(2,1)}, bf16[64,5120]{1,0:T(8,128)(2,1)}) custom-call(f32[8,640]{1,0:T(8,128)S(1)} %get-tuple-element.13.grad_first, f32[8,640]{1,0:T(8,128)S(1)} %get-tuple-element.14.grad_second, ...), custom_call_target="tpu_custom_call" | custom-call | flops 1509949440 | bytes 5898240 | tf_op jit(solution)/shard_map/weight_grads/pallas_call | solution.py:1006

commit v3 on v2

--- a/solution.py
+++ b/solution.py
@@ -62,6 +62,8 @@
         self.corners = corner
 
     def pick(self, values, kk, s):
+        if isinstance(kk, int):
+            return values[(kk + s) % 4]
         first, second = values[s % 4], values[(s + 1) % 4]
         return first + (second - first) * kk
 
@@ -230,24 +232,9 @@
 
 
 def lay_out(full, out, kk, core):
-    along_x = []
-    for x in range(4):
-        low, high = block_place(kk, x), block_place(2 + kk, x)
-        along_x.append(low + (high - low) * core)
-
-    def row(y):
-        yv = jnp.where(y >= 2, 1, 0)
-        y_low = y - 2 * yv
-        yu = y_low + yv - 2 * y_low * yv
-        weights = [(8 >> ((1 - k) % 4), 8 >> ((3 - k) % 4)) for k in (kk, 2 + kk)]
-        place_u = weights[0][0] + (weights[1][0] - weights[0][0]) * core
-        place_v = weights[0][1] + (weights[1][1] - weights[0][1]) * core
-        along_y = yu * place_u + yv * place_v
-        for x in range(4):
-            rows = pl.ds(pl.multiple_of(64 * y + 16 * x, 16), 16)
-            out[rows, slice_columns(kk, core)] = full[2 * core + kk, along_y + along_x[x]]
-
-    loop(0, 4, row)
+    for chip in range(CHIPS):
+        low, high = block_place(kk, chip), block_place(2 + kk, chip)
+        out[16 * chip : 16 * chip + 16, slice_columns(kk, core)] = full[2 * core + kk, low + (high - low) * core]
 
 
 REDUCE_SCRATCH = [
@@ -339,8 +326,7 @@
     def xy_start(self, kk, s, piece):
         self.xy_copy(kk, s, piece).start()
 
-    def plane(self, beside=None):
-        beside = beside or {}
+    def plane(self, own_part, beside):
         spot = self.spot
 
         def first(kk):
@@ -374,16 +360,25 @@
             own = spot.place(kk)
             self.tail_copy(kk, own + 1 - 2 * spot.bit(kk, 3), 1, spot.partner(kk, 3)).start()
 
-        loop(0, 2, first)
-        loop(0, 2, kept)
+        for kk in range(2):
+            own_part(kk, 0)
+            first(kk)
+        for kk in range(2):
+            own_part(kk, 1)
+        for kk in range(2):
+            kept(kk)
         for work in beside.get(-1, ()):
             work()
-        loop(0, 2, second)
-        loop(0, 2, lambda kk: arrive(kk, 0, 1))
+        for kk in range(2):
+            second(kk)
+        for kk in range(2):
+            arrive(kk, 0, 1)
         for work in beside.get(0, ()):
             work()
-        loop(0, 2, third)
-        loop(0, 2, fourth)
+        for kk in range(2):
+            third(kk)
+        for kk in range(2):
+            fourth(kk)
         for work in beside.get(1, ()):
             work()
         places = [spot.place(kk) for kk in range(2)]
@@ -643,7 +638,8 @@
             scale_ref[a, core] = jnp.broadcast_to(scales[core], (8, 128))
 
     def both(gather, stage):
-        loop(0, 2, lambda kk: gather.step(stage, kk))
+        for kk in range(2):
+            gather.step(stage, kk)
 
     send_raw(0, layer_out, raw_out)
     lax.fori_loop(1, 32, plane_start, 0)
@@ -651,10 +647,10 @@
     pass_raw(0, raw_out)
     normalise(0, raw_out, full_out, final_gain)
     both(gather_out, 0)
+    both(gather_out, 1)
     pass_raw(1, raw_mid)
-    both(gather_out, 1)
+    both(gather_out, 2)
     normalise(1, raw_mid, full_mid, mlp_gain)
-    both(gather_out, 2)
     both(gather_out, 3)
     both(gather_mid, 0)
 
@@ -675,7 +671,6 @@
     for kk in range(2):
         lay_out(full_out, final_rows, kk, other)
     products(final_rows, head, logits_ref, other)
-    both(gather_mid, 2)
 
     wait_bytes(got.at[pl.ds(0, 31)], plane_sems.at[1])
     logits = logits_ref[...]
@@ -698,7 +693,7 @@
             remote(first.at[0], first.at[2 * up + flip], stat_sems.at[0], stat_sems.at[1], target).start()
 
     loop(1, 8, to_column)
-    both(gather_mid, 3)
+    both(gather_mid, 2)
 
     def combine(ref, groups):
         top = ref[0, 0:1]
@@ -720,6 +715,7 @@
         remote(second.at[0], second.at[i], stat_sems.at[2], stat_sems.at[3], target).start()
 
     loop(1, CHIPS, to_plane)
+    both(gather_mid, 3)
     vocab = lax.broadcasted_iota(jnp.int32, (256, 384), 1) + (spot.z * 32 + spot.d) * 384
     stats_pad[...] = jnp.zeros_like(stats_pad)
     wait_bytes(second.at[pl.ds(1, 15)], stat_sems.at[3])
@@ -756,14 +752,13 @@
             spread(reduce, kk, other, (1 - sub) * (1 - bit) + sub * bit, left, right)
             reduce.start(kk, sub)
 
-        def to_self(i):
-            sub = jnp.where(i >= 2, 1, 0)
-            kk = i - 2 * sub
+        loop(0, 4, to_sibling)
+
+        def own_part(kk, sub):
             bit = spot.bit(kk, 0)
-            spread(reduce, kk, c, (1 - sub) * (1 - bit) + sub * bit, left, right)
-
-        loop(0, 4, to_sibling)
-        loop(0, 4, to_self)
+            spread(reduce, kk, c, (1 - bit) if sub == 0 else bit, left, right)
+
+        return own_part
 
     dlog_b = dlogits.astype(BF16)
     turn(dlog_b, dlog_turned)
@@ -793,8 +788,8 @@
     def turn_dlog():
         dlog_t[...] = jnp.transpose(dlog[...].astype(F32)).astype(BF16)
 
-    send_partial(reduces[0], dlog_turned, head)
-    sums = reduces[0].plane({-1: [mid_first], 0: [mid_second], 1: [activate]})
+    own_part = send_partial(reduces[0], dlog_turned, head)
+    sums = reduces[0].plane(own_part, {-1: [mid_first], 0: [mid_second], 1: [activate]})
     grad_out = reduces[0].column(sums, raw_out, final_gain, scale_ref[0, c][:, 0:1])
     own_b[...] = grad_out.astype(BF16)
     grad_first[...] = grad_out
@@ -839,20 +834,21 @@
     both_grads = jnp.concatenate([gate_grad, act * gate * gate_sigmoid], axis=0)
     turn(jnp.transpose(both_grads).astype(BF16), hidden_turned)
     hidden_t[...] = both_grads.astype(BF16)
-    send_partial(reduces[1], hidden_turned, w_gate_up)
-
-    for a in range(2):
-        wait_bytes(raw_out.at[pl.ds(0, 7)], raw_sems.at[a, 0])
-        wait_bytes(raw_out.at[pl.ds(0, 8)], raw_sems.at[a, 2])
-    wait_bytes(got.at[pl.ds(0, 31)], plane_sems.at[0])
-    wait_bytes(first.at[pl.ds(1, 15)], stat_sems.at[0])
-    wait_bytes(second.at[pl.ds(1, 15)], stat_sems.at[2])
-    for gather in gathers:
-        gather.finish()
-    reduces[0].finish()
-    wait_column(spot, own_from, own_sems.at[0])
-
-    sums = reduces[1].plane()
+    own_part = send_partial(reduces[1], hidden_turned, w_gate_up)
+
+    def left_earlier():
+        for a in range(2):
+            wait_bytes(raw_out.at[pl.ds(0, 7)], raw_sems.at[a, 0])
+            wait_bytes(raw_out.at[pl.ds(0, 8)], raw_sems.at[a, 2])
+        wait_bytes(got.at[pl.ds(0, 31)], plane_sems.at[0])
+        wait_bytes(first.at[pl.ds(1, 15)], stat_sems.at[0])
+        wait_bytes(second.at[pl.ds(1, 15)], stat_sems.at[2])
+        for gather in gathers:
+            gather.finish()
+        reduces[0].finish()
+        wait_column(spot, own_from, own_sems.at[0])
+
+    sums = reduces[1].plane(own_part, {-1: [left_earlier]})
     grad_second[...] = reduces[1].column(sums, raw_mid, mlp_gain, scale_ref[1, c][:, 0:1])
     reduces[1].finish()
 

time: 124 us -> 119 us (0.960)
  Pallas kernels: 124 us -> 118 us
    pallas_call x1, Pallas kernels: 120 us -> 114 us  [per_device(): pl.pallas_call(program, out_shape=[pltpu.VMEM((8, BLOCK), F32), pltpu.VME...]
where the time goes in v3:
time: 119 us
  Pallas kernels  118 us (99%)
    pallas_call x1, Pallas kernels, per_device(): pl.pallas_call(program, out_shape=[pltpu.VMEM((8, BLOCK), F32), pltpu.VME...  114 us
    pallas_call x1, Pallas kernels, per_device(): pl.pallas_call(weight_grads, out_shape=[shape((8, BLOCK), BF16), shape(he...  4.14 us

profile of v3, /device:TPU:1, one launch (start us, length us, event | category | flops | bytes accessed | tf_op | source)
XLA Modules:
  0.0 118.9 jit_solution(16850872187616633980)
XLA Ops:
  0.6 114.1 %backward.1 = (f32[8,640]{1,0:T(8,128)S(1)}, f32[8,640]{1,0:T(8,128)S(1)}, bf16[256,5120]{1,0:T(8,128)(2,1)S(1)}, bf16[256,5120]{1,0:T(8,128)(2,1)S(1)}, bf16[25...) custom-call(bf16[8,640]{1,0:T(8,128)(2,1)} %layer_out.1, ...), custom_call_target="tpu_custom_call" | custom-call | tf_op jit(solution)/shard_map/backward/pallas_call | solution.py:934
  114.8 4.1 %weight_grads.1 = (bf16[8,640]{1,0:T(8,128)(2,1)}, bf16[384,5120]{1,0:T(8,128)(2,1)}, bf16[64,5120]{1,0:T(8,128)(2,1)}, bf16[64,5120]{1,0:T(8,128)(2,1)}, bf16[64,5120]{1,0:T(8,128)(2,1)}) custom-call(f32[8,640]{1,0:T(8,128)S(1)} %get-tuple-element.13.grad_first, f32[8,640]{1,0:T(8,128)S(1)} %get-tuple-element.14.grad_second, ...), custom_call_target="tpu_custom_call" | custom-call | flops 1509949440 | bytes 5898240 | tf_op jit(solution)/shard_map/weight_grads/pallas_call | solution.py:1002

commit v4 on v3

--- a/solution.py
+++ b/solution.py
@@ -578,6 +578,47 @@
     raw_out[mine] = layer_out[...]
     raw_mid[mine] = resid_mid[...]
 
+    greeted()
+
+    def send_raw(a, own, raw):
+        loop(
+            1,
+            8,
+            lambda up: remote(
+                own, raw.at[mine], raw_sems.at[a, 0], raw_sems.at[a, 1], spot.column_peer(up)
+            ).start(),
+        )
+
+    def pass_raw(a, raw):
+        wait_bytes(raw.at[pl.ds(0, 7)], raw_sems.at[a, 1])
+        rows = raw.at[pl.ds(8 * c, 8)]
+        remote(rows, rows, raw_sems.at[a, 2], raw_sems.at[a, 3], spot.sibling()).start()
+
+    def plane_start(i, carry):
+        peer = wrap(spot.d + i, 32)
+        remote(packed.at[peer], got.at[spot.d], plane_sems.at[0], plane_sems.at[1], (peer, spot.z)).start()
+        return carry
+
+    def normalise(a, raw, full, gain):
+        wait_bytes(raw.at[pl.ds(0, 8)], raw_sems.at[a, 3])
+        scales = [row_scale(raw, core) for core in range(2)]
+        for kk in range(2):
+            place = spot.place(kk)
+            for j in range(2):
+                zb = 4 * c + 2 * kk + j
+                rows = jnp.concatenate(
+                    [raw[8 * core + zb].astype(F32) * scales[core] * gain[zb] for core in range(2)], axis=0
+                )
+                full[2 * c + kk, place, :, j * BLOCK : (j + 1) * BLOCK] = rows.astype(BF16)
+        for core in range(2):
+            scale_ref[a, core] = jnp.broadcast_to(scales[core], (8, 128))
+
+    def both(gather, stage):
+        for kk in range(2):
+            gather.step(stage, kk)
+
+    send_raw(0, layer_out, raw_out)
+
     row = lax.broadcasted_iota(jnp.int32, (8, 1), 0)
     order = jnp.zeros((8, 1), jnp.int32)
     for r in range(8):
@@ -602,51 +643,13 @@
         own_lengths = jnp.where(here, lengths[0, r // SLOT], own_lengths)
     live = (lax.rem(token, SLOT) < own_lengths).astype(jnp.int32)
     codes = jnp.where(own_ids >= 0, 2 * own_ids + live, 0).astype(F32)
-    greeted()
-
-    def send_raw(a, own, raw):
-        loop(
-            1,
-            8,
-            lambda up: remote(
-                own, raw.at[mine], raw_sems.at[a, 0], raw_sems.at[a, 1], spot.column_peer(up)
-            ).start(),
-        )
-
-    def pass_raw(a, raw):
-        wait_bytes(raw.at[pl.ds(0, 7)], raw_sems.at[a, 1])
-        rows = raw.at[pl.ds(8 * c, 8)]
-        remote(rows, rows, raw_sems.at[a, 2], raw_sems.at[a, 3], spot.sibling()).start()
-
-    def plane_start(i, carry):
-        peer = wrap(spot.d + i, 32)
-        remote(packed.at[peer], got.at[spot.d], plane_sems.at[0], plane_sems.at[1], (peer, spot.z)).start()
-        return carry
-
-    def normalise(a, raw, full, gain):
-        wait_bytes(raw.at[pl.ds(0, 8)], raw_sems.at[a, 3])
-        scales = [row_scale(raw, core) for core in range(2)]
-        for kk in range(2):
-            place = spot.place(kk)
-            for j in range(2):
-                zb = 4 * c + 2 * kk + j
-                rows = jnp.concatenate(
-                    [raw[8 * core + zb].astype(F32) * scales[core] * gain[zb] for core in range(2)], axis=0
-                )
-                full[2 * c + kk, place, :, j * BLOCK : (j + 1) * BLOCK] = rows.astype(BF16)
-        for core in range(2):
-            scale_ref[a, core] = jnp.broadcast_to(scales[core], (8, 128))
-
-    def both(gather, stage):
-        for kk in range(2):
-            gather.step(stage, kk)
-
-    send_raw(0, layer_out, raw_out)
-    lax.fori_loop(1, 32, plane_start, 0)
+
+    lax.fori_loop(1, 14, plane_start, 0)
     send_raw(1, resid_mid, raw_mid)
     pass_raw(0, raw_out)
     normalise(0, raw_out, full_out, final_gain)
     both(gather_out, 0)
+    lax.fori_loop(14, 32, plane_start, 0)
     both(gather_out, 1)
     pass_raw(1, raw_mid)
     both(gather_out, 2)
@@ -782,15 +785,18 @@
         products(w_gate_up, normed, gate_up_pre, other)
 
     def activate():
-        gate = gate_up_pre[0:64]
-        activated_t[...] = (gate * jax.nn.sigmoid(gate) * gate_up_pre[64:128]).astype(BF16)
+        gate, up = gate_up_pre[0:64], gate_up_pre[64:128]
+        gate_sigmoid = jax.nn.sigmoid(gate)
+        activated_t[...] = (gate * gate_sigmoid * up).astype(BF16)
+        gate_up_pre[0:64] = up * gate_sigmoid * (1.0 + gate * (1.0 - gate_sigmoid))
+        gate_up_pre[64:128] = gate * gate_sigmoid
 
     def turn_dlog():
         dlog_t[...] = jnp.transpose(dlog[...].astype(F32)).astype(BF16)
 
     own_part = send_partial(reduces[0], dlog_turned, head)
-    sums = reduces[0].plane(own_part, {-1: [mid_first], 0: [mid_second], 1: [activate]})
-    grad_out = reduces[0].column(sums, raw_out, final_gain, scale_ref[0, c][:, 0:1])
+    sums = reduces[0].plane(own_part, {-1: [turn_dlog]})
+    grad_out = reduces[0].column(sums, raw_out, final_gain, scale_ref[0, c][:, 0:1], [mid_first])
     own_b[...] = grad_out.astype(BF16)
     grad_first[...] = grad_out
 
@@ -810,7 +816,8 @@
             own_from[own_place] = own_b[...]
 
     loop(0, 8, own_to_column)
-    turn_dlog()
+    mid_second()
+    activate()
     wait_column(spot, own_from, own_sems.at[1])
     for kk in range(2):
         for j in range(2):
@@ -828,10 +835,8 @@
         lay_out(full_grad, grad_rows, kk, other)
     products(w_down, grad_rows, act_grad, other)
 
-    gate, up, act = gate_up_pre[0:64], gate_up_pre[64:128], act_grad[...]
-    gate_sigmoid = jax.nn.sigmoid(gate)
-    gate_grad = act * up * gate_sigmoid * (1.0 + gate * (1.0 - gate_sigmoid))
-    both_grads = jnp.concatenate([gate_grad, act * gate * gate_sigmoid], axis=0)
+    act = act_grad[...]
+    both_grads = jnp.concatenate([act * gate_up_pre[0:64], act * gate_up_pre[64:128]], axis=0)
     turn(jnp.transpose(both_grads).astype(BF16), hidden_turned)
     hidden_t[...] = both_grads.astype(BF16)
     own_part = send_partial(reduces[1], hidden_turned, w_gate_up)
@@ -848,8 +853,8 @@
         reduces[0].finish()
         wait_column(spot, own_from, own_sems.at[0])
 
-    sums = reduces[1].plane(own_part, {-1: [left_earlier]})
-    grad_second[...] = reduces[1].column(sums, raw_mid, mlp_gain, scale_ref[1, c][:, 0:1])
+    sums = reduces[1].plane(own_part, {})
+    grad_second[...] = reduces[1].column(sums, raw_mid, mlp_gain, scale_ref[1, c][:, 0:1], [left_earlier])
     reduces[1].finish()
 
 

time: 119 us -> 118 us (level)
  no operation moved by 1% of the time
where the time goes in v4:
time: 118 us
  Pallas kernels  118 us (100%)
    pallas_call x1, Pallas kernels, per_device(): pl.pallas_call(program, out_shape=[pltpu.VMEM((8, BLOCK), F32), pltpu.VME...  113 us
    pallas_call x1, Pallas kernels, per_device(): pl.pallas_call(weight_grads, out_shape=[shape((8, BLOCK), BF16), shape(he...  4.14 us

profile of v4, /device:TPU:1, one launch (start us, length us, event | category | flops | bytes accessed | tf_op | source)
XLA Modules:
  0.0 118.2 jit_solution(15326382632911067766)
XLA Ops:
  0.6 113.4 %backward.1 = (f32[8,640]{1,0:T(8,128)S(1)}, f32[8,640]{1,0:T(8,128)S(1)}, bf16[256,5120]{1,0:T(8,128)(2,1)S(1)}, bf16[256,5120]{1,0:T(8,128)(2,1)S(1)}, bf16[25...) custom-call(bf16[8,640]{1,0:T(8,128)(2,1)} %layer_out.1, ...), custom_call_target="tpu_custom_call" | custom-call | tf_op jit(solution)/shard_map/backward/pallas_call | solution.py:939
  114.0 4.1 %weight_grads.1 = (bf16[8,640]{1,0:T(8,128)(2,1)}, bf16[384,5120]{1,0:T(8,128)(2,1)}, bf16[64,5120]{1,0:T(8,128)(2,1)}, bf16[64,5120]{1,0:T(8,128)(2,1)}, bf16[64,5120]{1,0:T(8,128)(2,1)}) custom-call(f32[8,640]{1,0:T(8,128)S(1)} %get-tuple-element.13.grad_first, f32[8,640]{1,0:T(8,128)S(1)} %get-tuple-element.14.grad_second, ...), custom_call_target="tpu_custom_call" | custom-call | flops 1509949440 | bytes 5898240 | tf_op jit(solution)/shard_map/weight_grads/pallas_call | solution.py:1007

commit v5 on v4

--- a/solution.py
+++ b/solution.py
@@ -326,7 +326,8 @@
     def xy_start(self, kk, s, piece):
         self.xy_copy(kk, s, piece).start()
 
-    def plane(self, own_part, beside):
+    def plane(self, parts, beside):
+        sib_part, own_part = parts
         spot = self.spot
 
         def first(kk):
@@ -361,8 +362,12 @@
             self.tail_copy(kk, own + 1 - 2 * spot.bit(kk, 3), 1, spot.partner(kk, 3)).start()
 
         for kk in range(2):
+            sib_part(kk, 0)
+        for kk in range(2):
             own_part(kk, 0)
             first(kk)
+        for kk in range(2):
+            sib_part(kk, 1)
         for kk in range(2):
             own_part(kk, 1)
         for kk in range(2):
@@ -669,11 +674,11 @@
     loads[0].wait()
     logits_ref[...] = jnp.zeros_like(logits_ref)
     products(final_rows, head, logits_ref, c)
-    both(gather_mid, 1)
     both(gather_out, 4)
     for kk in range(2):
         lay_out(full_out, final_rows, kk, other)
     products(final_rows, head, logits_ref, other)
+    both(gather_mid, 1)
 
     wait_bytes(got.at[pl.ds(0, 31)], plane_sems.at[1])
     logits = logits_ref[...]
@@ -746,22 +751,18 @@
         part = jnp.dot(rows, right[:, slice_columns(kk, core)], preferred_element_type=F32).astype(BF16)
         reduce.partial[k, pl.ds(half * 8, 8)] = part.reshape(8, 16, SLICE)
 
-    def send_partial(reduce, left, right):
-
-        def to_sibling(i):
-            sub = jnp.where(i >= 2, 1, 0)
-            kk = i - 2 * sub
+    def partials(reduce, left, right):
+
+        def sib_part(kk, sub):
             bit = spot.sib_bit(kk, 0)
-            spread(reduce, kk, other, (1 - sub) * (1 - bit) + sub * bit, left, right)
+            spread(reduce, kk, other, (1 - bit) if sub == 0 else bit, left, right)
             reduce.start(kk, sub)
-
-        loop(0, 4, to_sibling)
 
         def own_part(kk, sub):
             bit = spot.bit(kk, 0)
             spread(reduce, kk, c, (1 - bit) if sub == 0 else bit, left, right)
 
-        return own_part
+        return sib_part, own_part
 
     dlog_b = dlogits.astype(BF16)
     turn(dlog_b, dlog_turned)
@@ -794,8 +795,7 @@
     def turn_dlog():
         dlog_t[...] = jnp.transpose(dlog[...].astype(F32)).astype(BF16)
 
-    own_part = send_partial(reduces[0], dlog_turned, head)
-    sums = reduces[0].plane(own_part, {-1: [turn_dlog]})
+    sums = reduces[0].plane(partials(reduces[0], dlog_turned, head), {-1: [turn_dlog]})
     grad_out = reduces[0].column(sums, raw_out, final_gain, scale_ref[0, c][:, 0:1], [mid_first])
     own_b[...] = grad_out.astype(BF16)
     grad_first[...] = grad_out
@@ -839,7 +839,6 @@
     both_grads = jnp.concatenate([act * gate_up_pre[0:64], act * gate_up_pre[64:128]], axis=0)
     turn(jnp.transpose(both_grads).astype(BF16), hidden_turned)
     hidden_t[...] = both_grads.astype(BF16)
-    own_part = send_partial(reduces[1], hidden_turned, w_gate_up)
 
     def left_earlier():
         for a in range(2):
@@ -853,7 +852,7 @@
         reduces[0].finish()
         wait_column(spot, own_from, own_sems.at[0])
 
-    sums = reduces[1].plane(own_part, {})
+    sums = reduces[1].plane(partials(reduces[1], hidden_turned, w_gate_up), {})
     grad_second[...] = reduces[1].column(sums, raw_mid, mlp_gain, scale_ref[1, c][:, 0:1], [left_earlier])
     reduces[1].finish()
 

time: 118 us -> 117 us (level)
  Pallas kernels: 118 us -> 116 us
    pallas_call x1, Pallas kernels: 113 us -> 112 us  [per_device(): pl.pallas_call(program, out_shape=[pltpu.VMEM((8, BLOCK), F32), pltpu.VME...]
where the time goes in v5:
time: 117 us
  Pallas kernels  116 us (99%)
    pallas_call x1, Pallas kernels, per_device(): pl.pallas_call(program, out_shape=[pltpu.VMEM((8, BLOCK), F32), pltpu.VME...  112 us
    pallas_call x1, Pallas kernels, per_device(): pl.pallas_call(weight_grads, out_shape=[shape((8, BLOCK), BF16), shape(he...  4.14 us

profile of v5, /device:TPU:1, one launch (start us, length us, event | category | flops | bytes accessed | tf_op | source)
XLA Modules:
  0.0 116.9 jit_solution(16301903417165532006)
XLA Ops:
  0.6 112.1 %backward.1 = (f32[8,640]{1,0:T(8,128)S(1)}, f32[8,640]{1,0:T(8,128)S(1)}, bf16[256,5120]{1,0:T(8,128)(2,1)S(1)}, bf16[256,5120]{1,0:T(8,128)(2,1)S(1)}, bf16[25...) custom-call(bf16[8,640]{1,0:T(8,128)(2,1)} %layer_out.1, ...), custom_call_target="tpu_custom_call" | custom-call | tf_op jit(solution)/shard_map/backward/pallas_call | solution.py:938
  112.7 4.1 %weight_grads.1 = (bf16[8,640]{1,0:T(8,128)(2,1)}, bf16[384,5120]{1,0:T(8,128)(2,1)}, bf16[64,5120]{1,0:T(8,128)(2,1)}, bf16[64,5120]{1,0:T(8,128)(2,1)}, bf16[64,5120]{1,0:T(8,128)(2,1)}) custom-call(f32[8,640]{1,0:T(8,128)S(1)} %get-tuple-element.13.grad_first, f32[8,640]{1,0:T(8,128)S(1)} %get-tuple-element.14.grad_second, ...), custom_call_target="tpu_custom_call" | custom-call | flops 1509949440 | bytes 5898240 | tf_op jit(solution)/shard_map/weight_grads/pallas_call | solution.py:1006

commit v6 on v5

--- a/solution.py
+++ b/solution.py
@@ -660,7 +660,6 @@
     both(gather_out, 2)
     normalise(1, raw_mid, full_mid, mlp_gain)
     both(gather_out, 3)
-    both(gather_mid, 0)
 
     def products(left, right, out, core):
         def body(kk):
@@ -674,11 +673,11 @@
     loads[0].wait()
     logits_ref[...] = jnp.zeros_like(logits_ref)
     products(final_rows, head, logits_ref, c)
+    both(gather_mid, 0)
     both(gather_out, 4)
     for kk in range(2):
         lay_out(full_out, final_rows, kk, other)
     products(final_rows, head, logits_ref, other)
-    both(gather_mid, 1)
 
     wait_bytes(got.at[pl.ds(0, 31)], plane_sems.at[1])
     logits = logits_ref[...]
@@ -701,19 +700,19 @@
             remote(first.at[0], first.at[2 * up + flip], stat_sems.at[0], stat_sems.at[1], target).start()
 
     loop(1, 8, to_column)
-    both(gather_mid, 2)
+    both(gather_mid, 1)
+
+    place = lax.broadcasted_iota(jnp.int32, (4, 256), 0)
 
     def combine(ref, groups):
         top = ref[0, 0:1]
         for i in range(1, 16):
             top = jnp.maximum(top, ref[i, 0:1])
-        total = jnp.zeros_like(top)
-        moment = jnp.zeros_like(top)
+        sums = jnp.zeros((4, 256), F32)
         for i in range(16):
-            weight = jnp.exp(ref[i, 0:1] - top)
-            total = total + ref[i, 1:2] * weight
-            moment = moment + ref[i, 2:3] * weight
-        return jnp.concatenate([top, total, moment, sum(ref[i, 3:4] for i in range(groups))], axis=0)
+            sums = sums + ref[i] * jnp.exp(ref[i, 0:1] - top)
+        coded = sum(ref[i] for i in range(groups))
+        return jnp.where(place == 0, top, jnp.where(place == 3, coded, sums))
 
     wait_bytes(first.at[pl.ds(1, 15)], stat_sems.at[1])
     second[0] = combine(first, 2)
@@ -723,7 +722,7 @@
         remote(second.at[0], second.at[i], stat_sems.at[2], stat_sems.at[3], target).start()
 
     loop(1, CHIPS, to_plane)
-    both(gather_mid, 3)
+    both(gather_mid, 2)
     vocab = lax.broadcasted_iota(jnp.int32, (256, 384), 1) + (spot.z * 32 + spot.d) * 384
     stats_pad[...] = jnp.zeros_like(stats_pad)
     wait_bytes(second.at[pl.ds(1, 15)], stat_sems.at[3])
@@ -780,6 +779,9 @@
         mid_rows(c)
         products(w_gate_up, normed, gate_up_pre, c)
 
+    def mid_third():
+        both(gather_mid, 3)
+
     def mid_second():
         both(gather_mid, 4)
         mid_rows(other)
@@ -795,8 +797,8 @@
     def turn_dlog():
         dlog_t[...] = jnp.transpose(dlog[...].astype(F32)).astype(BF16)
 
-    sums = reduces[0].plane(partials(reduces[0], dlog_turned, head), {-1: [turn_dlog]})
-    grad_out = reduces[0].column(sums, raw_out, final_gain, scale_ref[0, c][:, 0:1], [mid_first])
+    sums = reduces[0].plane(partials(reduces[0], dlog_turned, head), {})
+    grad_out = reduces[0].column(sums, raw_out, final_gain, scale_ref[0, c][:, 0:1], [mid_third, mid_first, turn_dlog])
     own_b[...] = grad_out.astype(BF16)
     grad_first[...] = grad_out
 
@@ -882,7 +884,7 @@
     grad_resid[...] = (grad_first[...] + grad_second[...]).astype(BF16)
 
     def copies(k):
-        place = pl.ds(pl.multiple_of(k * SLICE, SLICE), SLICE)
+        place = pl.ds(pl.multiple_of(k * BLOCK, BLOCK), BLOCK)
         return [
             pltpu.make_async_copy(head_rows.at[:, place], grad_head.at[:, place], sems.at[0, k]),
             pltpu.make_async_copy(gate_up_rows.at[pl.ds(0, 64), place], grad_gate.at[:, place], sems.at[1, k]),
@@ -891,7 +893,7 @@
         ]
 
     def chunk(k):
-        place = pl.ds(pl.multiple_of(k * SLICE, SLICE), SLICE)
+        place = pl.ds(pl.multiple_of(k * BLOCK, BLOCK), BLOCK)
         to_head, to_gate, to_up, to_down = copies(k)
         head_rows[:, place] = product(dlog_t[...], final_rows[:, place])
         to_head.start()
@@ -905,8 +907,8 @@
         for copy in copies(k):
             copy.wait()
 
-    loop(0, 4, chunk)
-    loop(0, 4, done)
+    loop(0, 8, chunk)
+    loop(0, 8, done)
 
 
 def shape(dims, dtype):
@@ -1018,7 +1020,7 @@
             pltpu.VMEM((384, D), BF16),
             pltpu.VMEM((128, D), BF16),
             pltpu.VMEM((64, D), BF16),
-            dma((4, 4)),
+            dma((4, 8)),
         ],
         compiler_params=pltpu.CompilerParams(vmem_limit_bytes=GRADS_VMEM),
         cost_estimate=pl.CostEstimate(flops=2 * 256 * 576 * D, bytes_accessed=2 * 576 * D, transcendentals=0),

time: 117 us -> 115 us (0.983)
    pallas_call x1, Pallas kernels: 112 us -> 110 us  [per_device(): pl.pallas_call(program, out_shape=[pltpu.VMEM((8, BLOCK), F32), pltpu.VME...]
where the time goes in v6:
time: 115 us
  Pallas kernels  115 us (100%)
    pallas_call x1, Pallas kernels, per_device(): pl.pallas_call(program, out_shape=[pltpu.VMEM((8, BLOCK), F32), pltpu.VME...  110 us
    pallas_call x1, Pallas kernels, per_device(): pl.pallas_call(weight_grads, out_shape=[shape((8, BLOCK), BF16), shape(he...  4.93 us

profile of v6, /device:TPU:1, one launch (start us, length us, event | category | flops | bytes accessed | tf_op | source)
XLA Modules:
  0.0 115.4 jit_solution(6457574926427742090)
XLA Ops:
  0.6 109.8 %backward.1 = (f32[8,640]{1,0:T(8,128)S(1)}, f32[8,640]{1,0:T(8,128)S(1)}, bf16[256,5120]{1,0:T(8,128)(2,1)S(1)}, bf16[256,5120]{1,0:T(8,128)(2,1)S(1)}, bf16[25...) custom-call(bf16[8,640]{1,0:T(8,128)(2,1)} %layer_out.1, ...), custom_call_target="tpu_custom_call" | custom-call | tf_op jit(solution)/shard_map/backward/pallas_call | solution.py:940
  110.4 4.9 %weight_grads.1 = (bf16[8,640]{1,0:T(8,128)(2,1)}, bf16[384,5120]{1,0:T(8,128)(2,1)}, bf16[64,5120]{1,0:T(8,128)(2,1)}, bf16[64,5120]{1,0:T(8,128)(2,1)}, bf16[64,5120]{1,0:T(8,128)(2,1)}) custom-call(f32[8,640]{1,0:T(8,128)S(1)} %get-tuple-element.13.grad_first, f32[8,640]{1,0:T(8,128)S(1)} %get-tuple-element.14.grad_second, ...), custom_call_target="tpu_custom_call" | custom-call | flops 1509949440 | bytes 5898240 | tf_op jit(solution)/shard_map/weight_grads/pallas_call | solution.py:1008

commit v7 on v6

--- a/solution.py
+++ b/solution.py
@@ -884,7 +884,7 @@
     grad_resid[...] = (grad_first[...] + grad_second[...]).astype(BF16)
 
     def copies(k):
-        place = pl.ds(pl.multiple_of(k * BLOCK, BLOCK), BLOCK)
+        place = pl.ds(pl.multiple_of(k * SLICE, SLICE), SLICE)
         return [
             pltpu.make_async_copy(head_rows.at[:, place], grad_head.at[:, place], sems.at[0, k]),
             pltpu.make_async_copy(gate_up_rows.at[pl.ds(0, 64), place], grad_gate.at[:, place], sems.at[1, k]),
@@ -893,7 +893,7 @@
         ]
 
     def chunk(k):
-        place = pl.ds(pl.multiple_of(k * BLOCK, BLOCK), BLOCK)
+        place = pl.ds(pl.multiple_of(k * SLICE, SLICE), SLICE)
         to_head, to_gate, to_up, to_down = copies(k)
         head_rows[:, place] = product(dlog_t[...], final_rows[:, place])
         to_head.start()
@@ -907,8 +907,8 @@
         for copy in copies(k):
             copy.wait()
 
-    loop(0, 8, chunk)
-    loop(0, 8, done)
+    loop(0, 4, chunk)
+    loop(0, 4, done)
 
 
 def shape(dims, dtype):
@@ -1020,7 +1020,7 @@
             pltpu.VMEM((384, D), BF16),
             pltpu.VMEM((128, D), BF16),
             pltpu.VMEM((64, D), BF16),
-            dma((4, 8)),
+            dma((4, 4)),
         ],
         compiler_params=pltpu.CompilerParams(vmem_limit_bytes=GRADS_VMEM),
         cost_estimate=pl.CostEstimate(flops=2 * 256 * 576 * D, bytes_accessed=2 * 576 * D, transcendentals=0),

time: 115 us -> 115 us (level)
  no operation moved by 1% of the time
where the time goes in v7:
time: 115 us
  Pallas kernels  114 us (99%)
    pallas_call x1, Pallas kernels, per_device(): pl.pallas_call(program, out_shape=[pltpu.VMEM((8, BLOCK), F32), pltpu.VME...  110 us
    pallas_call x1, Pallas kernels, per_device(): pl.pallas_call(weight_grads, out_shape=[shape((8, BLOCK), BF16), shape(he...  4.14 us

profile of v7, /device:TPU:1, one launch (start us, length us, event | category | flops | bytes accessed | tf_op | source)
XLA Modules:
  0.0 114.6 jit_solution(14761475159336200750)
XLA Ops:
  0.6 109.8 %backward.1 = (f32[8,640]{1,0:T(8,128)S(1)}, f32[8,640]{1,0:T(8,128)S(1)}, bf16[256,5120]{1,0:T(8,128)(2,1)S(1)}, bf16[256,5120]{1,0:T(8,128)(2,1)S(1)}, bf16[25...) custom-call(bf16[8,640]{1,0:T(8,128)(2,1)} %layer_out.1, ...), custom_call_target="tpu_custom_call" | custom-call | tf_op jit(solution)/shard_map/backward/pallas_call | solution.py:940
  110.5 4.1 %weight_grads.1 = (bf16[8,640]{1,0:T(8,128)(2,1)}, bf16[384,5120]{1,0:T(8,128)(2,1)}, bf16[64,5120]{1,0:T(8,128)(2,1)}, bf16[64,5120]{1,0:T(8,128)(2,1)}, bf16[64,5120]{1,0:T(8,128)(2,1)}) custom-call(f32[8,640]{1,0:T(8,128)S(1)} %get-tuple-element.13.grad_first, f32[8,640]{1,0:T(8,128)S(1)} %get-tuple-element.14.grad_second, ...), custom_call_target="tpu_custom_call" | custom-call | flops 1509949440 | bytes 5898240 | tf_op jit(solution)/shard_map/weight_grads/pallas_call | solution.py:1008
